TPU v7x, 32 devices: a whole 2x2x4 slice. The times are simulated.
32 devices in a mesh: seq: 4 (over y, x), ctx: 8 (over z, core).
Axes of the slice: x: 2, y: 2, z: 4, core: 2. Of those that a mesh axis runs over, the one named last changes fastest.
Arguments:
- tokens: bfloat16 [16, 768, 768], P('seq', 'ctx'), may hold values from -6 to 6
- query_key_value_matrix: bfloat16 [768, 2304], P('seq'), may hold values from -0.21875 to 0.21875
- attention_output_matrix: bfloat16 [768, 768], P('seq'), may hold values from -6 to 6
- gate_up_matrix: bfloat16 [768, 2304], P('seq'), may hold values from -0.21875 to 0.21875
- feedforward_output_matrix: bfloat16 [1152, 768], P('seq'), may hold values from -0.1875 to 0.1875
- gain_attn: bfloat16 [768], P('seq'), may hold values from 0.099609375 to 1.8984375
- gain_mlp: bfloat16 [768], P('seq'), may hold values from 0.099609375 to 1.8984375
- cotangent: bfloat16 [16, 768, 768], P('seq', 'ctx'), may hold values from -6 to 6
Outputs:
- layer_output: bfloat16 [16, 768, 768], P('seq', 'ctx')
- grad_tokens: float32 [16, 768, 768], P('seq', 'ctx')
- grad_w_qkv: float32 [768, 2304], P('seq')
- grad_w_attn_out: float32 [768, 768], P('seq')
- grad_w_in: float32 [768, 2304], P('seq')
- grad_w_mlp_out: float32 [1152, 768], P('seq')
- grad_gain_attn: float32 [768], P('seq')
- grad_gain_mlp: float32 [768], P('seq')
All inputs are finite; a program needn't handle non-finite values.
Results may differ from a plain program's by a relative error of at most 0.024.
Values may be sent and summed in bfloat16 or wider, within the bound.
A program may use at most 192 MiB of HBM per device.

v0:
```python
import jax
import jax.numpy as jnp
from jax import lax
from jax.sharding import PartitionSpec as P

H = 12
HD = 64
FF = 1152


rope_base = 160000.0
norm_eps = 1e-05


def from_behind(block, axis, distance):
    devices = range(lax.axis_size(axis))
    route = [((i - distance) % len(devices), i) for i in devices]
    return lax.ppermute(block, axis, route)


def layer_norm(values_in, gain_vector):
    average = jnp.mean(values_in, axis=-1, keepdims=True)
    centred = values_in - average
    variance = jnp.mean(centred * centred, axis=-1, keepdims=True)
    return centred * lax.rsqrt(variance + norm_eps) * gain_vector


def angle_tables(positions):
    half_size = HD // 2
    frequency = rope_base ** (-(jnp.arange(half_size, dtype=jnp.float32) * 2.0) / HD)
    angles = positions[:, None] * frequency[None, :]
    angles = jnp.concatenate([angles, angles], axis=-1)
    return (jnp.cos(angles), jnp.sin(angles))


def rotate(heads, cosine_table, sine_table):
    half_size = heads.shape[-1] // 2
    front_half = heads[..., :half_size]
    back_half = heads[..., half_size:]
    turned = jnp.concatenate([-back_half, front_half], axis=-1)
    return heads * cosine_table[:, None, :] + turned * sine_table[:, None, :]


def unrotate(grads_in, cosine_table, sine_table):
    half_size = grads_in.shape[-1] // 2
    scaled = grads_in * sine_table[:, None, :]
    turned = jnp.concatenate([scaled[..., half_size:], -scaled[..., :half_size]], axis=-1)
    return grads_in * cosine_table[:, None, :] + turned


def gated_unit(gate_part, up_part):
    return jax.nn.gelu(gate_part, approximate=False) * up_part


def pass_grads(stacked_grads):
    return from_behind(stacked_grads.astype(jnp.bfloat16), "ctx", 1).astype(stacked_grads.dtype)


def body(
    tokens,
    query_key_value_matrix,
    attention_output_matrix,
    gate_up_matrix,
    feedforward_output_matrix,
    gain_attn,
    gain_mlp,
    cotangent,
):
    (
        query_key_value_weight,
        attention_output_weight,
        gate_up_weight,
        feedforward_output_weight,
        gain_one,
        gain_two,
    ) = (
        lax.all_gather(query_key_value_matrix, "seq", axis=0, tiled=True),
        lax.all_gather(attention_output_matrix, "seq", axis=0, tiled=True),
        lax.all_gather(gate_up_matrix, "seq", axis=0, tiled=True),
        lax.all_gather(feedforward_output_matrix, "seq", axis=0, tiled=True),
        lax.all_gather(gain_attn, "seq", axis=0, tiled=True),
        lax.all_gather(gain_mlp, "seq", axis=0, tiled=True),
    )
    seqs_here, block_rows, model_width = tokens.shape
    head_shape = (seqs_here, block_rows, H, HD)
    flat_shape = (seqs_here, block_rows, model_width)
    single_float = jnp.float32
    bf16 = jnp.bfloat16
    inputs = tokens.astype(single_float)
    ln_one, ln_one_back = jax.vjp(layer_norm, inputs, gain_one.astype(single_float))
    first_normalized = ln_one.astype(bf16)
    query_key_value = jnp.einsum(
        "jka,an->jkn", first_normalized, query_key_value_weight, preferred_element_type=single_float
    )
    positions = (
        lax.axis_index("ctx") * block_rows + jnp.arange(block_rows, dtype=jnp.int32)
    ).astype(single_float)
    cosine_table, sine_table = angle_tables(positions)
    queries = rotate(
        query_key_value[..., :model_width].reshape(head_shape), cosine_table, sine_table
    ).astype(bf16)
    key_heads = rotate(
        query_key_value[..., model_width : 2 * model_width].reshape(head_shape),
        cosine_table,
        sine_table,
    ).astype(bf16)
    value_heads = query_key_value[..., 2 * model_width :].reshape(head_shape).astype(bf16)
    send_keys = key_heads.reshape(flat_shape)
    send_values = value_heads.reshape(flat_shape)
    pieces = (
        lax.all_gather(send_keys, "ctx", axis=1, tiled=True),
        lax.all_gather(send_values, "ctx", axis=1, tiled=True),
    )
    running = jnp.full((seqs_here, H, block_rows), -1e30, single_float)
    rows_in = pieces[0].shape[1]
    key_rows = pieces[0].reshape(seqs_here, rows_in, H, HD)
    value_rows = pieces[1].reshape(seqs_here, rows_in, H, HD)
    scores = (
        jnp.einsum("sqhd,skhd->shqk", queries, key_rows, preferred_element_type=single_float)
        * 0.125
    )
    newest = jnp.maximum(running, jnp.max(scores, axis=-1))
    weights_here = jnp.exp(scores - newest[..., None])
    summed = jnp.sum(weights_here, axis=-1)
    accumulated = jnp.einsum(
        "shqk,skhd->shqd",
        weights_here.astype(bf16),
        value_rows,
        preferred_element_type=single_float,
    )
    running, summed, accumulated = (newest, summed, accumulated)
    log_total = running + jnp.log(summed)
    attention_result = jnp.transpose(accumulated / summed[..., None], (0, 2, 1, 3))
    attention_result_lowered = attention_result.reshape(flat_shape).astype(bf16)
    residual_branch = jnp.einsum(
        "jka,an->jkn",
        attention_result_lowered,
        attention_output_weight,
        preferred_element_type=single_float,
    )
    middle = inputs + residual_branch
    ln_two, ln_two_back = jax.vjp(layer_norm, middle, gain_two.astype(single_float))
    second_normalized = ln_two.astype(bf16)
    gate_up_product = jnp.einsum(
        "uvc,cw->uvw", second_normalized, gate_up_weight, preferred_element_type=single_float
    )
    mixed_hidden_state, gated_back = jax.vjp(
        gated_unit, gate_up_product[..., :FF], gate_up_product[..., FF:]
    )
    mixed_hidden_lowered = mixed_hidden_state.astype(bf16)
    feedforward_output = jnp.einsum(
        "umz,zy->umy",
        mixed_hidden_lowered,
        feedforward_output_weight,
        preferred_element_type=single_float,
    )
    layer_output = (middle + feedforward_output).astype(bf16)
    upstream = cotangent.astype(single_float)
    feedforward_output_weight_gradient = jnp.einsum(
        "nzh,nzx->hx", mixed_hidden_lowered, cotangent, preferred_element_type=single_float
    )
    mixed_hidden_gradient = jnp.einsum(
        "kic,gc->kig", cotangent, feedforward_output_weight, preferred_element_type=single_float
    )
    grad_gate, grad_up = gated_back(mixed_hidden_gradient)
    gate_up_product_gradient = jnp.concatenate([grad_gate, grad_up], axis=-1).astype(bf16)
    gate_up_weight_gradient = jnp.einsum(
        "nkb,nkp->bp",
        second_normalized,
        gate_up_product_gradient,
        preferred_element_type=single_float,
    )
    second_normalized_gradient = jnp.einsum(
        "axo,eo->axe", gate_up_product_gradient, gate_up_weight, preferred_element_type=single_float
    )
    grad_middle_norm, grad_gain_two = ln_two_back(second_normalized_gradient)
    grad_middle = upstream + grad_middle_norm
    residual_branch_gradient = grad_middle.astype(bf16)
    attention_output_weight_gradient = jnp.einsum(
        "xwn,xwp->np",
        attention_result_lowered,
        residual_branch_gradient,
        preferred_element_type=single_float,
    )
    grad_attended = jnp.einsum(
        "onc,jc->onj",
        residual_branch_gradient,
        attention_output_weight,
        preferred_element_type=single_float,
    ).astype(bf16)
    grad_heads = grad_attended.reshape(head_shape)
    row_delta = jnp.transpose(
        jnp.sum(grad_heads.astype(single_float) * attention_result, axis=-1), (0, 2, 1)
    )

    def block_grads(stacked_blocks, stacked_grads, grad_q):
        key_rows = stacked_blocks[0].reshape(head_shape)
        value_rows = stacked_blocks[1].reshape(head_shape)
        scores = (
            jnp.einsum("sqhd,skhd->shqk", queries, key_rows, preferred_element_type=single_float)
            * 0.125
        )
        probabilities = jnp.exp(scores - log_total[..., None])
        grad_probs = jnp.einsum(
            "sqhd,skhd->shqk", grad_heads, value_rows, preferred_element_type=single_float
        )
        grad_scores = (probabilities * (grad_probs - row_delta[..., None])).astype(bf16)
        grad_q = grad_q + jnp.einsum(
            "shqk,skhd->sqhd", grad_scores, key_rows, preferred_element_type=single_float
        )
        grad_k_term = jnp.einsum(
            "shqk,sqhd->skhd", grad_scores, queries, preferred_element_type=single_float
        )
        grad_v_term = jnp.einsum(
            "shqk,sqhd->skhd",
            probabilities.astype(bf16),
            grad_heads,
            preferred_element_type=single_float,
        )
        stacked_grads = stacked_grads + jnp.stack([grad_k_term, grad_v_term])
        return (stacked_grads, grad_q)

    def cycle_step(step_index, carried):
        stacked_blocks, stacked_grads, grad_q = carried
        stacked_grads, grad_q = block_grads(stacked_blocks, stacked_grads, grad_q)
        stacked_blocks = from_behind(stacked_blocks, "ctx", 1)
        stacked_grads = pass_grads(stacked_grads)
        return (stacked_blocks, stacked_grads, grad_q)

    cycle_count = lax.axis_size("ctx")
    start_cycle = (
        jnp.stack([send_keys, send_values]),
        jnp.zeros((2,) + head_shape, single_float),
        jnp.zeros(head_shape, single_float),
    )
    stacked_blocks, stacked_grads, grad_q = lax.fori_loop(
        0, cycle_count - 1, cycle_step, start_cycle
    )
    stacked_grads, grad_q = block_grads(stacked_blocks, stacked_grads, grad_q)
    stacked_grads = pass_grads(stacked_grads)
    grad_queries = grad_q * 0.125
    grad_keys = stacked_grads[0]
    grad_values = stacked_grads[1]
    grad_keys = grad_keys * 0.125
    query_key_value_gradient = jnp.concatenate(
        [
            unrotate(grad_queries, cosine_table, sine_table).reshape(flat_shape),
            unrotate(grad_keys, cosine_table, sine_table).reshape(flat_shape),
            grad_values.reshape(flat_shape),
        ],
        axis=-1,
    ).astype(bf16)
    query_key_value_weight_gradient = jnp.einsum(
        "xwn,xwp->np",
        first_normalized,
        query_key_value_gradient,
        preferred_element_type=single_float,
    )
    first_normalized_gradient = jnp.einsum(
        "onc,jc->onj",
        query_key_value_gradient,
        query_key_value_weight,
        preferred_element_type=single_float,
    )
    grad_inputs_norm, grad_gain_one = ln_one_back(first_normalized_gradient)
    grad_inputs = grad_middle + grad_inputs_norm
    summed_all = (
        lax.psum(query_key_value_weight_gradient.astype(jnp.bfloat16), "ctx").astype(jnp.float32),
        lax.psum(attention_output_weight_gradient.astype(jnp.bfloat16), "ctx").astype(jnp.float32),
        lax.psum(gate_up_weight_gradient.astype(jnp.bfloat16), "ctx").astype(jnp.float32),
        lax.psum(feedforward_output_weight_gradient.astype(jnp.bfloat16), "ctx").astype(
            jnp.float32
        ),
        lax.psum(grad_gain_one.astype(jnp.bfloat16), "ctx").astype(jnp.float32),
        lax.psum(grad_gain_two.astype(jnp.bfloat16), "ctx").astype(jnp.float32),
    )
    shards = (
        lax.psum_scatter(
            summed_all[0].astype(jnp.bfloat16), "seq", scatter_dimension=0, tiled=True
        ).astype(jnp.float32),
        lax.psum_scatter(
            summed_all[1].astype(jnp.bfloat16), "seq", scatter_dimension=0, tiled=True
        ).astype(jnp.float32),
        lax.psum_scatter(
            summed_all[2].astype(jnp.bfloat16), "seq", scatter_dimension=0, tiled=True
        ).astype(jnp.float32),
        lax.psum_scatter(
            summed_all[3].astype(jnp.bfloat16), "seq", scatter_dimension=0, tiled=True
        ).astype(jnp.float32),
        lax.psum_scatter(
            summed_all[4].astype(jnp.bfloat16), "seq", scatter_dimension=0, tiled=True
        ).astype(jnp.float32),
        lax.psum_scatter(
            summed_all[5].astype(jnp.bfloat16), "seq", scatter_dimension=0, tiled=True
        ).astype(jnp.float32),
    )
    return (
        layer_output,
        grad_inputs,
        shards[0],
        shards[1],
        shards[2],
        shards[3],
        shards[4],
        shards[5],
    )


def solution(mesh):
    placed = (
        P("seq", "ctx", None),
        P("seq", None),
        P("seq", None),
        P("seq", None),
        P("seq", None),
        P("seq"),
        P("seq"),
        P("seq", "ctx", None),
    )
    return jax.shard_map(
        body,
        mesh=mesh,
        in_specs=placed,
        out_specs=(
            P("seq", "ctx", None),
            P("seq", "ctx", None),
            P("seq", None),
            P("seq", None),
            P("seq", None),
            P("seq", None),
            P("seq"),
            P("seq"),
        ),
        check_vma=False,
    )
```

profile of v0, /device:TPU:0, one launch (start us, length us, event | category | flops | bytes accessed | tf_op | source)
XLA Modules:
  0.0 855.3 jit_solution(8972303702187118788)
XLA Ops:
  11.6 11.3 %all-reduce.7 = (bf16[768]{0:T(1024)(128)(2,1)S(1)}, bf16[768]{0:T(1024)(128)(2,1)S(1)}) all-reduce(bf16[768]{0:T(1024)(128)(2,1)S(1)} %dynamic-update-slice, bf16[768]{0:T(1024)(128)(2,1)S(1)} %dynamic-update-slice.1), channel_id=1, replica_groups=mesh['seq'=4,'ctx'=8] {'seq'}, use_global_device_ids=true, to_apply=%add | all-reduce | flops 1536 | bytes 6144
  24.7 35.1 %all-gather.7.cloned.1.call-done = bf16[768,2304]{1,0:T(8,128)(2,1)} async-done(((bf16[192,2304]{1,0:T(8,128)(2,1)}), bf16[768,2304]{1,0:T(8,128)(2,1)}) %all-gather.7.cloned.1.call-update) | async-done | bytes 3538960 | tf_op jit(solution)/shard_map/all_gather | solution.py:77
  80.8 44.4 %all-gather.9.cloned.1.call-done = bf16[4,768,768]{2,1,0:T(8,128)(2,1)} async-done(((bf16[4,96,768]{2,1,0:T(8,128)(2,1)}), bf16[4,768,768]{2,1,0:T(8,128)(2,1)}) %all-gather.9.cloned.1.call-update) | async-done | bytes 4718608 | tf_op jit(solution)/shard_map/all_gather | solution.py:111
  125.3 6.6 copy.55
  145.0 33.0 %all-gather.11.cloned.1.call-done = bf16[4,768,768]{2,1,0:T(8,128)(2,1)} async-done(((bf16[4,96,768]{2,1,0:T(8,128)(2,1)}), bf16[4,768,768]{2,1,0:T(8,128)(2,1)}) %all-gather.11.cloned.1.call-update) | async-done | bytes 4718608 | tf_op jit(solution)/shard_map/all_gather | solution.py:112
  178.0 6.6 copy.56
  184.7 11.0 %fusion.81 = (bf16[4,96,12,64]{1,3,2,0:T(8,128)(2,1)S(1)}, f32[4,96,12,64]{1,3,2,0:T(8,128)}) fusion(f32[4,96,12]{1,2,0:T(8,128)S(1)} %bitcast.173, bf16[4,768,12,64]{1,3,2,0:T(8,128)(2,1)} %bitcast.163, f32[4,12,96,768]{3,2,1,0:T(8,128)} %copy-done.6, f32[4,12,96]{2,1,0:T(8,128)S(1)} %broadcast_maximum_fusion), kind=kOutput, calls=%fused_computation.147 | convolution fusion | flops 464191488 | bytes 20680704 | tf_op jit(solution)/shard_map/shqk,skhd->shqd/dot_general | solution.py:125
  195.6 10.7 %all-gather.13.cloned.1.call-done = bf16[768,768]{1,0:T(8,128)(2,1)} async-done(((bf16[192,768]{1,0:T(8,128)(2,1)}), bf16[768,768]{1,0:T(8,128)(2,1)}) %all-gather.13.cloned.1.call-update) | async-done | bytes 1179664 | tf_op jit(solution)/shard_map/all_gather | solution.py:78
  208.7 46.6 %all-gather.15.cloned.1.call-done = bf16[768,2304]{1,0:T(8,128)(2,1)} async-done(((bf16[192,2304]{1,0:T(8,128)(2,1)}), bf16[768,2304]{1,0:T(8,128)(2,1)}) %all-gather.15.cloned.1.call-update) | async-done | bytes 3538960 | tf_op jit(solution)/shard_map/all_gather | solution.py:79
  255.3 5.4 fusion.14
  260.7 29.0 %all-gather.17.cloned.1.call-done = bf16[1152,768]{1,0:T(8,128)(2,1)} async-done(((bf16[288,768]{1,0:T(8,128)(2,1)}), bf16[1152,768]{1,0:T(8,128)(2,1)}) %all-gather.17.cloned.1.call-update) | async-done | bytes 1769488 | tf_op jit(solution)/shard_map/all_gather | solution.py:80
  289.6 7.1 add_convert_fusion
  321.1 358.0 %while.15 = (s32[]{:T(128)}, bf16[2,4,96,768]{3,2,1,0:T(8,128)(2,1)}, f32[2,4,96,12,64]{2,4,3,1,0:T(8,128)}, f32[4,96,12,64]{1,3,2,0:T(8,128)}, bf16[4,96,12,64]...) while((s32[]{:T(128)}, ...), condition=%wide.region_10.0_spmd.clone, body=%wide.region_9.0_spmd.clone.sunk | while | flops 290193408 | bytes 54761856 | solution.py:236
  340.8 18.2 %collective-permute-done.1 = bf16[2,4,96,12,64]{2,4,3,1,0:T(8,128)(2,1)} collective-permute-done((bf16[2,4,96,12,64]{2,4,3,1,0:T(8,128)(2,1)}, bf16[2,4,96,12,64]{2,4,3,1,0:T(8,128)(2,1)}, u32[]{:S(2)}, u32[]{:S(2)}) %collective-permute-start.1) | collective-permute-done | bytes 1179680 | tf_op jit(solution)/shard_map/while/body/eval_jaxpr/ppermute | solution.py:18
  362.5 9.2 %collective-permute-done = bf16[2,4,96,768]{3,2,1,0:T(8,128)(2,1)} collective-permute-done((bf16[2,4,96,768]{3,2,1,0:T(8,128)(2,1)}, bf16[2,4,96,768]{3,2,1,0:T(8,128)(2,1)}, u32[]{:S(2)}, u32[]{:S(2)}) %collective-permute-start) | collective-permute-done | bytes 1179680 | tf_op jit(solution)/shard_map/while/body/eval_jaxpr/ppermute | solution.py:18
  392.0 18.2 %collective-permute-done.1 = bf16[2,4,96,12,64]{2,4,3,1,0:T(8,128)(2,1)} collective-permute-done((bf16[2,4,96,12,64]{2,4,3,1,0:T(8,128)(2,1)}, bf16[2,4,96,12,64]{2,4,3,1,0:T(8,128)(2,1)}, u32[]{:S(2)}, u32[]{:S(2)}) %collective-permute-start.1) | collective-permute-done | bytes 1179680 | tf_op jit(solution)/shard_map/while/body/eval_jaxpr/ppermute | solution.py:18
  413.8 9.2 %collective-permute-done = bf16[2,4,96,768]{3,2,1,0:T(8,128)(2,1)} collective-permute-done((bf16[2,4,96,768]{3,2,1,0:T(8,128)(2,1)}, bf16[2,4,96,768]{3,2,1,0:T(8,128)(2,1)}, u32[]{:S(2)}, u32[]{:S(2)}) %collective-permute-start) | collective-permute-done | bytes 1179680 | tf_op jit(solution)/shard_map/while/body/eval_jaxpr/ppermute | solution.py:18
  443.1 18.4 %collective-permute-done.1 = bf16[2,4,96,12,64]{2,4,3,1,0:T(8,128)(2,1)} collective-permute-done((bf16[2,4,96,12,64]{2,4,3,1,0:T(8,128)(2,1)}, bf16[2,4,96,12,64]{2,4,3,1,0:T(8,128)(2,1)}, u32[]{:S(2)}, u32[]{:S(2)}) %collective-permute-start.1) | collective-permute-done | bytes 1179680 | tf_op jit(solution)/shard_map/while/body/eval_jaxpr/ppermute | solution.py:18
  465.0 9.2 %collective-permute-done = bf16[2,4,96,768]{3,2,1,0:T(8,128)(2,1)} collective-permute-done((bf16[2,4,96,768]{3,2,1,0:T(8,128)(2,1)}, bf16[2,4,96,768]{3,2,1,0:T(8,128)(2,1)}, u32[]{:S(2)}, u32[]{:S(2)}) %collective-permute-start) | collective-permute-done | bytes 1179680 | tf_op jit(solution)/shard_map/while/body/eval_jaxpr/ppermute | solution.py:18
  494.4 18.4 %collective-permute-done.1 = bf16[2,4,96,12,64]{2,4,3,1,0:T(8,128)(2,1)} collective-permute-done((bf16[2,4,96,12,64]{2,4,3,1,0:T(8,128)(2,1)}, bf16[2,4,96,12,64]{2,4,3,1,0:T(8,128)(2,1)}, u32[]{:S(2)}, u32[]{:S(2)}) %collective-permute-start.1) | collective-permute-done | bytes 1179680 | tf_op jit(solution)/shard_map/while/body/eval_jaxpr/ppermute | solution.py:18
  516.2 9.2 %collective-permute-done = bf16[2,4,96,768]{3,2,1,0:T(8,128)(2,1)} collective-permute-done((bf16[2,4,96,768]{3,2,1,0:T(8,128)(2,1)}, bf16[2,4,96,768]{3,2,1,0:T(8,128)(2,1)}, u32[]{:S(2)}, u32[]{:S(2)}) %collective-permute-start) | collective-permute-done | bytes 1179680 | tf_op jit(solution)/shard_map/while/body/eval_jaxpr/ppermute | solution.py:18
  545.6 18.4 %collective-permute-done.1 = bf16[2,4,96,12,64]{2,4,3,1,0:T(8,128)(2,1)} collective-permute-done((bf16[2,4,96,12,64]{2,4,3,1,0:T(8,128)(2,1)}, bf16[2,4,96,12,64]{2,4,3,1,0:T(8,128)(2,1)}, u32[]{:S(2)}, u32[]{:S(2)}) %collective-permute-start.1) | collective-permute-done | bytes 1179680 | tf_op jit(solution)/shard_map/while/body/eval_jaxpr/ppermute | solution.py:18
  567.5 9.2 %collective-permute-done = bf16[2,4,96,768]{3,2,1,0:T(8,128)(2,1)} collective-permute-done((bf16[2,4,96,768]{3,2,1,0:T(8,128)(2,1)}, bf16[2,4,96,768]{3,2,1,0:T(8,128)(2,1)}, u32[]{:S(2)}, u32[]{:S(2)}) %collective-permute-start) | collective-permute-done | bytes 1179680 | tf_op jit(solution)/shard_map/while/body/eval_jaxpr/ppermute | solution.py:18
  596.9 18.4 %collective-permute-done.1 = bf16[2,4,96,12,64]{2,4,3,1,0:T(8,128)(2,1)} collective-permute-done((bf16[2,4,96,12,64]{2,4,3,1,0:T(8,128)(2,1)}, bf16[2,4,96,12,64]{2,4,3,1,0:T(8,128)(2,1)}, u32[]{:S(2)}, u32[]{:S(2)}) %collective-permute-start.1) | collective-permute-done | bytes 1179680 | tf_op jit(solution)/shard_map/while/body/eval_jaxpr/ppermute | solution.py:18
  618.7 9.2 %collective-permute-done = bf16[2,4,96,768]{3,2,1,0:T(8,128)(2,1)} collective-permute-done((bf16[2,4,96,768]{3,2,1,0:T(8,128)(2,1)}, bf16[2,4,96,768]{3,2,1,0:T(8,128)(2,1)}, u32[]{:S(2)}, u32[]{:S(2)}) %collective-permute-start) | collective-permute-done | bytes 1179680 | tf_op jit(solution)/shard_map/while/body/eval_jaxpr/ppermute | solution.py:18
  648.1 18.4 %collective-permute-done.1 = bf16[2,4,96,12,64]{2,4,3,1,0:T(8,128)(2,1)} collective-permute-done((bf16[2,4,96,12,64]{2,4,3,1,0:T(8,128)(2,1)}, bf16[2,4,96,12,64]{2,4,3,1,0:T(8,128)(2,1)}, u32[]{:S(2)}, u32[]{:S(2)}) %collective-permute-start.1) | collective-permute-done | bytes 1179680 | tf_op jit(solution)/shard_map/while/body/eval_jaxpr/ppermute | solution.py:18
  670.0 9.2 %collective-permute-done = bf16[2,4,96,768]{3,2,1,0:T(8,128)(2,1)} collective-permute-done((bf16[2,4,96,768]{3,2,1,0:T(8,128)(2,1)}, bf16[2,4,96,768]{3,2,1,0:T(8,128)(2,1)}, u32[]{:S(2)}, u32[]{:S(2)}) %collective-permute-start) | collective-permute-done | bytes 1179680 | tf_op jit(solution)/shard_map/while/body/eval_jaxpr/ppermute | solution.py:18
  692.4 19.3 %collective-permute-done.2 = bf16[2,4,96,12,64]{2,4,3,1,0:T(8,128)(2,1)} collective-permute-done((bf16[2,4,96,12,64]{2,4,3,1,0:T(8,128)(2,1)}, bf16[2,4,96,12,64]{2,4,3,1,0:T(8,128)(2,1)}, u32[]{:S(2)}, u32[]{:S(2)}) %collective-permute-start.2) | collective-permute-done | bytes 1179680 | tf_op jit(solution)/shard_map/ppermute | solution.py:18
  731.5 39.9 %reduce-scatter.5.cloned.1.call-done = bf16[192,2304]{1,0:T(8,128)(2,1)} async-done(((bf16[768,2304]{1,0:T(8,128)(2,1)}), bf16[192,2304]{1,0:T(8,128)(2,1)}) %reduce-scatter.5.cloned.1.call-update) | async-done | bytes 884752 | tf_op jit(solution)/shard_map/reduce_scatter | solution.py:278
  776.4 9.6 %all-reduce.6 = (bf16[768]{0:T(1024)(128)(2,1)}, bf16[768]{0:T(1024)(128)(2,1)}) all-reduce(bf16[768]{0:T(1024)(128)(2,1)} %get-tuple-element.100, bf16[768]{0:T(1024)(128)(2,1)} %get-tuple-element.98), channel_id=6, replica_groups=mesh['seq'=4,'ctx'=8] {'seq'}, use_global_device_ids=true, to_apply=%region_23.0.clone | all-reduce | flops 1536 | bytes 6144
  788.5 15.7 %all-reduce.4 = (bf16[192]{0:T(256)(128)(2,1)}, bf16[192]{0:T(256)(128)(2,1)}) all-reduce(bf16[192]{0:T(256)(128)(2,1)} %dynamic-slice.3, bf16[192]{0:T(256)(128)(2,1)} %dynamic-slice.5), channel_id=1, replica_groups=mesh['seq'=4,'ctx'=8] {'ctx'}, use_global_device_ids=true, to_apply=%region_22.0 | all-reduce | flops 384 | bytes 1536 | tf_op jit(solution)/shard_map/psum | solution.py:274
  809.6 33.2 %all-reduce.10.cloned.1.call-done = (bf16[192,2304]{1,0:T(8,128)(2,1)}, bf16[192,768]{1,0:T(8,128)(2,1)}, bf16[192,2304]{1,0:T(8,128)(2,1)}, bf16[288,768]{1,0:T(8,128)(2,1)}) async-done(((bf16[192,2304]{1,0:T(8,128)(2,1)}, bf16[192,768]{1,0:T(8,128)(2,1)}, bf16[192,2304]{1,0:T(8,128)(2,1)}, bf16[288,768]{1,0:T(8,128)(2,1)}), (bf16[192,2304]{1,0:T(8,128)(2,1)}, bf16[192,768]{1,0:T(8,128)(2,1)}, ...) | async-done | bytes 2506768 | tf_op jit(solution)/shard_map/psum | solution.py:268
  (400 shorter events, 281.3 us)
Async XLA Ops:
  7.2 52.7 %all-gather.7.cloned.1.call-start = ((), (), s32[]{:S(2)}) async-start(), calls=%async_computation.4 | async-start | bytes 4423680 | tf_op jit(solution)/shard_map/all_gather | solution.py:77
  7.9 117.4 %all-gather.9.cloned.1.call-start = ((), (), s32[]{:S(2)}) async-start(), calls=%async_computation.5 | async-start | bytes 5308416 | tf_op jit(solution)/shard_map/all_gather | solution.py:111
  73.5 104.6 %all-gather.11.cloned.1.call-start = ((), (), s32[]{:S(2)}) async-start(), calls=%async_computation.6 | async-start | bytes 5308416 | tf_op jit(solution)/shard_map/all_gather | solution.py:112
  75.7 130.6 %all-gather.13.cloned.1.call-start = ((), (), s32[]{:S(2)}) async-start(), calls=%async_computation.7 | async-start | bytes 1474560 | tf_op jit(solution)/shard_map/all_gather | solution.py:78
  76.3 179.0 %all-gather.15.cloned.1.call-start = ((), (), s32[]{:S(2)}) async-start(), calls=%async_computation.8 | async-start | bytes 4423680 | tf_op jit(solution)/shard_map/all_gather | solution.py:79
  76.8 212.8 %all-gather.17.cloned.1.call-start = ((), (), s32[]{:S(2)}) async-start(), calls=%async_computation.9 | async-start | bytes 2211840 | tf_op jit(solution)/shard_map/all_gather | solution.py:80
  77.4 654.0 %reduce-scatter.7.cloned.1.call-start = ((), (), s32[]{:S(2)}) async-start(), calls=%async_computation.11 | async-start | bytes 1474560 | tf_op jit(solution)/shard_map/reduce_scatter | solution.py:281
  206.3 49.0 %copy-start.48 = (f32[768]{0:T(1024)S(1)}, f32[768]{0:T(1024)}, u32[]{:S(2)}) copy-start(f32[768]{0:T(1024)} %convert_element_type.147) | copy-start | bytes 9220
  208.3 108.7 %copy-start.10 = (f32[4,96,768]{2,1,0:T(8,128)}, f32[4,96,768]{2,1,0:T(8,128)S(1)}, u32[]{:S(2)}) copy-start(f32[4,96,768]{2,1,0:T(8,128)S(1)} %get-tuple-element.163) | copy-start | bytes 3538948
  208.4 93.7 %copy-start.44 = (f32[4,96]{1,0:T(4,128)}, f32[4,96]{1,0:T(4,128)S(1)}, u32[]{:S(2)}) copy-start(f32[4,96]{1,0:T(4,128)S(1)} %broadcast_multiply_fusion.4) | copy-start | bytes 4612
  208.7 93.4 %copy-start.50 = (f32[4,96]{1,0:T(4,128)}, f32[4,96]{1,0:T(4,128)S(1)}, u32[]{:S(2)}) copy-start(f32[4,96]{1,0:T(4,128)S(1)} %fusion.67) | copy-start | bytes 4612
  208.7 81.0 %copy-start.20 = (bf16[4,96,768]{2,1,0:T(8,128)(2,1)S(1)}, bf16[4,96,768]{2,1,0:T(8,128)(2,1)}, u32[]{:S(2)}) copy-start(bf16[4,96,768]{2,1,0:T(8,128)(2,1)} %param.17) | copy-start | bytes 1769476
  306.6 424.9 %reduce-scatter.11.cloned.1.call-start = ((), (), s32[]{:S(2)}) async-start(), calls=%async_computation.13 | async-start | bytes 2211840 | tf_op jit(solution)/shard_map/reduce_scatter | solution.py:287
  310.1 421.3 %reduce-scatter.9.cloned.1.call-start = ((), (), s32[]{:S(2)}) async-start(), calls=%async_computation.12 | async-start | bytes 4423680 | tf_op jit(solution)/shard_map/reduce_scatter | solution.py:284
  321.1 450.3 %reduce-scatter.5.cloned.1.call-start = ((), (), s32[]{:S(2)}) async-start(), calls=%async_computation.10 | async-start | bytes 4423680 | tf_op jit(solution)/shard_map/reduce_scatter | solution.py:278
  337.1 22.0 %collective-permute-start.1 = (bf16[2,4,96,12,64]{2,4,3,1,0:T(8,128)(2,1)}, bf16[2,4,96,12,64]{2,4,3,1,0:T(8,128)(2,1)}, u32[]{:S(2)}, u32[]{:S(2)}) collective-permute-start(bf16[2,4,96,12,64]{2,4,3,1,0:T(8,128)(2,1)} %fusion.139), channel_id=1, source_target_pairs={{7,0},{0,1},{1,2},{2,3},{3,4},{4,5},{5,6},{6,7},{15,8},{8,9},{9,10... | collective-permute-start | bytes 3538952 | tf_op jit(solution)/shard_map/while/body/eval_jaxpr/ppermute | solution.py:18
  337.1 34.6 %collective-permute-start = (bf16[2,4,96,768]{3,2,1,0:T(8,128)(2,1)}, bf16[2,4,96,768]{3,2,1,0:T(8,128)(2,1)}, u32[]{:S(2)}, u32[]{:S(2)}) collective-permute-start(bf16[2,4,96,768]{3,2,1,0:T(8,128)(2,1)} %copy.80), channel_id=1, source_target_pairs={{7,0},{0,1},{1,2},{2,3},{3,4},{4,5},{5,6},{6,7},{15,8},{8,9},{9,10... | collective-permute-start | bytes 3538952 | tf_op jit(solution)/shard_map/while/body/eval_jaxpr/ppermute | solution.py:18
  388.3 22.0 %collective-permute-start.1 = (bf16[2,4,96,12,64]{2,4,3,1,0:T(8,128)(2,1)}, bf16[2,4,96,12,64]{2,4,3,1,0:T(8,128)(2,1)}, u32[]{:S(2)}, u32[]{:S(2)}) collective-permute-start(bf16[2,4,96,12,64]{2,4,3,1,0:T(8,128)(2,1)} %fusion.139), channel_id=1, source_target_pairs={{7,0},{0,1},{1,2},{2,3},{3,4},{4,5},{5,6},{6,7},{15,8},{8,9},{9,10... | collective-permute-start | bytes 3538952 | tf_op jit(solution)/shard_map/while/body/eval_jaxpr/ppermute | solution.py:18
  388.3 34.6 %collective-permute-start = (bf16[2,4,96,768]{3,2,1,0:T(8,128)(2,1)}, bf16[2,4,96,768]{3,2,1,0:T(8,128)(2,1)}, u32[]{:S(2)}, u32[]{:S(2)}) collective-permute-start(bf16[2,4,96,768]{3,2,1,0:T(8,128)(2,1)} %copy.80), channel_id=1, source_target_pairs={{7,0},{0,1},{1,2},{2,3},{3,4},{4,5},{5,6},{6,7},{15,8},{8,9},{9,10... | collective-permute-start | bytes 3538952 | tf_op jit(solution)/shard_map/while/body/eval_jaxpr/ppermute | solution.py:18
  439.6 22.0 %collective-permute-start.1 = (bf16[2,4,96,12,64]{2,4,3,1,0:T(8,128)(2,1)}, bf16[2,4,96,12,64]{2,4,3,1,0:T(8,128)(2,1)}, u32[]{:S(2)}, u32[]{:S(2)}) collective-permute-start(bf16[2,4,96,12,64]{2,4,3,1,0:T(8,128)(2,1)} %fusion.139), channel_id=1, source_target_pairs={{7,0},{0,1},{1,2},{2,3},{3,4},{4,5},{5,6},{6,7},{15,8},{8,9},{9,10... | collective-permute-start | bytes 3538952 | tf_op jit(solution)/shard_map/while/body/eval_jaxpr/ppermute | solution.py:18
  439.6 34.6 %collective-permute-start = (bf16[2,4,96,768]{3,2,1,0:T(8,128)(2,1)}, bf16[2,4,96,768]{3,2,1,0:T(8,128)(2,1)}, u32[]{:S(2)}, u32[]{:S(2)}) collective-permute-start(bf16[2,4,96,768]{3,2,1,0:T(8,128)(2,1)} %copy.80), channel_id=1, source_target_pairs={{7,0},{0,1},{1,2},{2,3},{3,4},{4,5},{5,6},{6,7},{15,8},{8,9},{9,10... | collective-permute-start | bytes 3538952 | tf_op jit(solution)/shard_map/while/body/eval_jaxpr/ppermute | solution.py:18
  490.8 22.0 %collective-permute-start.1 = (bf16[2,4,96,12,64]{2,4,3,1,0:T(8,128)(2,1)}, bf16[2,4,96,12,64]{2,4,3,1,0:T(8,128)(2,1)}, u32[]{:S(2)}, u32[]{:S(2)}) collective-permute-start(bf16[2,4,96,12,64]{2,4,3,1,0:T(8,128)(2,1)} %fusion.139), channel_id=1, source_target_pairs={{7,0},{0,1},{1,2},{2,3},{3,4},{4,5},{5,6},{6,7},{15,8},{8,9},{9,10... | collective-permute-start | bytes 3538952 | tf_op jit(solution)/shard_map/while/body/eval_jaxpr/ppermute | solution.py:18
  490.8 34.6 %collective-permute-start = (bf16[2,4,96,768]{3,2,1,0:T(8,128)(2,1)}, bf16[2,4,96,768]{3,2,1,0:T(8,128)(2,1)}, u32[]{:S(2)}, u32[]{:S(2)}) collective-permute-start(bf16[2,4,96,768]{3,2,1,0:T(8,128)(2,1)} %copy.80), channel_id=1, source_target_pairs={{7,0},{0,1},{1,2},{2,3},{3,4},{4,5},{5,6},{6,7},{15,8},{8,9},{9,10... | collective-permute-start | bytes 3538952 | tf_op jit(solution)/shard_map/while/body/eval_jaxpr/ppermute | solution.py:18
  542.0 22.0 %collective-permute-start.1 = (bf16[2,4,96,12,64]{2,4,3,1,0:T(8,128)(2,1)}, bf16[2,4,96,12,64]{2,4,3,1,0:T(8,128)(2,1)}, u32[]{:S(2)}, u32[]{:S(2)}) collective-permute-start(bf16[2,4,96,12,64]{2,4,3,1,0:T(8,128)(2,1)} %fusion.139), channel_id=1, source_target_pairs={{7,0},{0,1},{1,2},{2,3},{3,4},{4,5},{5,6},{6,7},{15,8},{8,9},{9,10... | collective-permute-start | bytes 3538952 | tf_op jit(solution)/shard_map/while/body/eval_jaxpr/ppermute | solution.py:18
  542.0 34.6 %collective-permute-start = (bf16[2,4,96,768]{3,2,1,0:T(8,128)(2,1)}, bf16[2,4,96,768]{3,2,1,0:T(8,128)(2,1)}, u32[]{:S(2)}, u32[]{:S(2)}) collective-permute-start(bf16[2,4,96,768]{3,2,1,0:T(8,128)(2,1)} %copy.80), channel_id=1, source_target_pairs={{7,0},{0,1},{1,2},{2,3},{3,4},{4,5},{5,6},{6,7},{15,8},{8,9},{9,10... | collective-permute-start | bytes 3538952 | tf_op jit(solution)/shard_map/while/body/eval_jaxpr/ppermute | solution.py:18
  593.3 22.0 %collective-permute-start.1 = (bf16[2,4,96,12,64]{2,4,3,1,0:T(8,128)(2,1)}, bf16[2,4,96,12,64]{2,4,3,1,0:T(8,128)(2,1)}, u32[]{:S(2)}, u32[]{:S(2)}) collective-permute-start(bf16[2,4,96,12,64]{2,4,3,1,0:T(8,128)(2,1)} %fusion.139), channel_id=1, source_target_pairs={{7,0},{0,1},{1,2},{2,3},{3,4},{4,5},{5,6},{6,7},{15,8},{8,9},{9,10... | collective-permute-start | bytes 3538952 | tf_op jit(solution)/shard_map/while/body/eval_jaxpr/ppermute | solution.py:18
  593.3 34.6 %collective-permute-start = (bf16[2,4,96,768]{3,2,1,0:T(8,128)(2,1)}, bf16[2,4,96,768]{3,2,1,0:T(8,128)(2,1)}, u32[]{:S(2)}, u32[]{:S(2)}) collective-permute-start(bf16[2,4,96,768]{3,2,1,0:T(8,128)(2,1)} %copy.80), channel_id=1, source_target_pairs={{7,0},{0,1},{1,2},{2,3},{3,4},{4,5},{5,6},{6,7},{15,8},{8,9},{9,10... | collective-permute-start | bytes 3538952 | tf_op jit(solution)/shard_map/while/body/eval_jaxpr/ppermute | solution.py:18
  644.5 22.0 %collective-permute-start.1 = (bf16[2,4,96,12,64]{2,4,3,1,0:T(8,128)(2,1)}, bf16[2,4,96,12,64]{2,4,3,1,0:T(8,128)(2,1)}, u32[]{:S(2)}, u32[]{:S(2)}) collective-permute-start(bf16[2,4,96,12,64]{2,4,3,1,0:T(8,128)(2,1)} %fusion.139), channel_id=1, source_target_pairs={{7,0},{0,1},{1,2},{2,3},{3,4},{4,5},{5,6},{6,7},{15,8},{8,9},{9,10... | collective-permute-start | bytes 3538952 | tf_op jit(solution)/shard_map/while/body/eval_jaxpr/ppermute | solution.py:18
  644.5 34.6 %collective-permute-start = (bf16[2,4,96,768]{3,2,1,0:T(8,128)(2,1)}, bf16[2,4,96,768]{3,2,1,0:T(8,128)(2,1)}, u32[]{:S(2)}, u32[]{:S(2)}) collective-permute-start(bf16[2,4,96,768]{3,2,1,0:T(8,128)(2,1)} %copy.80), channel_id=1, source_target_pairs={{7,0},{0,1},{1,2},{2,3},{3,4},{4,5},{5,6},{6,7},{15,8},{8,9},{9,10... | collective-permute-start | bytes 3538952 | tf_op jit(solution)/shard_map/while/body/eval_jaxpr/ppermute | solution.py:18
  689.5 22.2 %collective-permute-start.2 = (bf16[2,4,96,12,64]{2,4,3,1,0:T(8,128)(2,1)}, bf16[2,4,96,12,64]{2,4,3,1,0:T(8,128)(2,1)}, u32[]{:S(2)}, u32[]{:S(2)}) collective-permute-start(bf16[2,4,96,12,64]{2,4,3,1,0:T(8,128)(2,1)} %fusion.21), channel_id=1, source_target_pairs={{7,0},{0,1},{1,2},{2,3},{3,4},{4,5},{5,6},{6,7},{15,8},{8,9},{9,10... | collective-permute-start | bytes 3538952 | tf_op jit(solution)/shard_map/ppermute | solution.py:18
  726.7 116.1 %all-reduce.10.cloned.1.call-start = ((), (), s32[]{:S(2)}) async-start(), calls=%async_computation.14 | async-start | bytes 5013504 | tf_op jit(solution)/shard_map/psum | solution.py:268
  731.4 40.0 %copy-start.32 = (bf16[4,96,768]{2,1,0:T(8,128)(2,1)S(1)}, bf16[4,96,768]{2,1,0:T(8,128)(2,1)}, u32[]{:S(2)}) copy-start(bf16[4,96,768]{2,1,0:T(8,128)(2,1)} %copy.65) | copy-start | bytes 1769476
  (91 other events, 882.2 us)
Sparse Core Ops, SparseCore 0:
  9.9 49.9 all-gather.6
  73.6 51.6 all-gather.8
  127.5 50.5 all-gather.10
  179.7 26.5 all-gather.12
  208.0 47.2 all-gather.14
  257.0 32.5 all-gather.16
  306.7 28.5 reduce-scatter.6
  338.9 32.4 reduce-scatter.10
  374.5 47.1 reduce-scatter.8
  726.8 44.5 reduce-scatter.4
  774.0 68.6 all-reduce.9
where the time goes:
time: 862 us; the launch traced here: 855 us
  waiting for transfers between devices  486 us (56%)
  matrix products  131 us (15%)
  local copies, waits for them, and re-layouts  94.2 us (11%)
  other arithmetic  87.4 us (10%)
  blocking collectives  36.7 us (4%)
  between operations  16.3 us (2%)
    ppermute x15, waiting for transfers between devices, from_behind(): return lax.ppermute(block, axis, route)  212 us
    all_gather x1, waiting for transfers between devices, body(): lax.all_gather(gate_up_matrix, 'seq', axis=0, tiled=True)  46.6 us
    all_gather x1, waiting for transfers between devices, body(): lax.all_gather(send_keys, 'ctx', axis=1, tiled=True)  44.4 us
    reduce_scatter x1, waiting for transfers between devices, body(): lax.psum_scatter(summed_all[0].astype(jnp.bfloat16), 'seq', scatter_dimen...  39.9 us
    all_gather x1, waiting for transfers between devices, body(): lax.all_gather(query_key_value_matrix, 'seq', axis=0, tiled=True)  35.1 us
    psum x1, waiting for transfers between devices, body(): lax.psum(query_key_value_weight_gradient.astype(jnp.bfloat16), 'ctx')  33.2 us
    all_gather x1, waiting for transfers between devices, body(): lax.all_gather(send_values, 'ctx', axis=1, tiled=True)  33 us
    convert_element_type x8, other arithmetic, pass_grads(): stacked_grads.astype(jnp.bfloat16)  30.8 us
  transfers between devices with their start and end apart: 26, of which 23 were waited for; matrix products, arithmetic and copies ran while one was open for 31% of the time, Pallas kernels for 0%

commit v1 on v0

v1 whole, which is shorter than its diff:
```python
import functools

import jax
import jax.numpy as jnp
from jax import lax
from jax.experimental import pallas as pl
from jax.experimental.pallas import tpu as pltpu
from jax.sharding import PartitionSpec as P

H = 12
HD = 64
FF = 1152
PAIR = 2 * HD

rope_base = 160000.0
norm_eps = 1e-05
f32 = jnp.float32
bf16 = jnp.bfloat16


def dot(a, b, dims):
    return lax.dot_general(a, b, (dims, ((), ())), preferred_element_type=f32)


NN = ((1,), (0,))
NT = ((1,), (1,))
TN = ((0,), (0,))


def attend_kernel(q_ref, k_ref, v_ref, o_ref, lse_ref):
    outs, totals = [], []
    for half in range(2):
        cols = slice(half * HD, (half + 1) * HD)
        scores = dot(q_ref[:, cols], k_ref[:, cols], NT) * 0.125
        largest = jnp.max(scores, axis=-1, keepdims=True)
        weights = jnp.exp(scores - largest)
        total = jnp.sum(weights, axis=-1, keepdims=True)
        outs.append(dot(weights.astype(bf16), v_ref[:, cols], NN) / total)
        totals.append(jnp.broadcast_to(largest + jnp.log(total), outs[-1].shape))
    o_ref[...] = jnp.concatenate(outs, axis=-1).astype(bf16)
    lse_ref[...] = jnp.concatenate(totals, axis=-1)


def attend_back_kernel(q_ref, k_ref, v_ref, do_ref, lse_ref, dq_ref, dk_ref, dv_ref):
    dqs, dks, dvs = [], [], []
    for half in range(2):
        cols = slice(half * HD, (half + 1) * HD)
        q, k, v, do = q_ref[:, cols], k_ref[:, cols], v_ref[:, cols], do_ref[:, cols]
        scores = dot(q, k, NT) * 0.125
        probabilities = jnp.exp(scores - lse_ref[:, half * HD : half * HD + 1])
        grad_probs = dot(do, v, NT)
        delta = jnp.sum(probabilities * grad_probs, axis=-1, keepdims=True)
        grad_scores = (probabilities * (grad_probs - delta)).astype(bf16)
        dqs.append(dot(grad_scores, k, NN) * 0.125)
        dks.append(dot(grad_scores, q, TN) * 0.125)
        dvs.append(dot(probabilities.astype(bf16), do, TN))
    dq_ref[...] = jnp.concatenate(dqs, axis=-1)
    dk_ref[...] = jnp.concatenate(dks, axis=-1).astype(bf16)
    dv_ref[...] = jnp.concatenate(dvs, axis=-1).astype(bf16)


def column_blocks(rows):
    return pl.BlockSpec((rows, PAIR), lambda h: (0, h))


def attend(q, k, v):
    rows, width = q.shape
    keys = k.shape[0]
    return pl.pallas_call(
        attend_kernel,
        grid=(width // PAIR,),
        in_specs=[column_blocks(rows), column_blocks(keys), column_blocks(keys)],
        out_specs=[column_blocks(rows), column_blocks(rows)],
        out_shape=[
            jax.ShapeDtypeStruct((rows, width), bf16),
            jax.ShapeDtypeStruct((rows, width), f32),
        ],
        compiler_params=pltpu.CompilerParams(vmem_limit_bytes=50 * 2**20),
        cost_estimate=pl.CostEstimate(
            flops=4 * rows * keys * width,
            bytes_accessed=8 * (rows + keys) * width,
            transcendentals=rows * keys * H,
        ),
    )(q, k, v)


def attend_back(q, k, v, do, lse):
    rows, width = q.shape
    keys = k.shape[0]
    return pl.pallas_call(
        attend_back_kernel,
        grid=(width // PAIR,),
        in_specs=[
            column_blocks(rows),
            column_blocks(keys),
            column_blocks(keys),
            column_blocks(rows),
            column_blocks(rows),
        ],
        out_specs=[column_blocks(rows), column_blocks(keys), column_blocks(keys)],
        out_shape=[
            jax.ShapeDtypeStruct((rows, width), f32),
            jax.ShapeDtypeStruct((keys, width), bf16),
            jax.ShapeDtypeStruct((keys, width), bf16),
        ],
        compiler_params=pltpu.CompilerParams(vmem_limit_bytes=50 * 2**20),
        cost_estimate=pl.CostEstimate(
            flops=10 * rows * keys * width,
            bytes_accessed=12 * (rows + keys) * width,
            transcendentals=rows * keys * H,
        ),
    )(q, k, v, do, lse)


def turn(values):
    column = lax.broadcasted_iota(jnp.int32, values.shape, 1)
    ahead = jnp.concatenate([values[:, HD // 2 :], values[:, : HD // 2]], axis=1)
    behind = jnp.concatenate([values[:, -(HD // 2) :], values[:, : -(HD // 2)]], axis=1)
    return jnp.where(column % HD < HD // 2, -ahead, behind)


def rotate(values, cosines, sines):
    return values * cosines + turn(values) * sines


def unrotate(values, cosines, sines):
    return values * cosines - turn(values * sines)


def normalize(values):
    average = jnp.mean(values, axis=-1, keepdims=True)
    centred = values - average
    variance = jnp.mean(centred * centred, axis=-1, keepdims=True)
    scale = lax.rsqrt(variance + norm_eps)
    return centred * scale, scale


def norm_back(e, xhat, scale):
    return scale * (
        e - jnp.mean(e, axis=-1, keepdims=True) - xhat * jnp.mean(e * xhat, axis=-1, keepdims=True)
    )


def body(seqs_here, group, tokens, w_qkv, w_attn, w_in, w_mlp, gain_one, gain_two, cotangent):
    block_rows, width = tokens.shape[1:]
    ctx = seqs_here * group
    me = lax.axis_index("ctx")
    mine, place = me // group, me % group

    def hop(block, distance):
        route = [(i, (i + distance * group) % ctx) for i in range(ctx)]
        return lax.ppermute(block, "ctx", route)

    def to_sequence(values):
        parts = [lax.dynamic_index_in_dim(values, mine, 0, keepdims=False)]
        for d in range(1, seqs_here):
            part = lax.dynamic_index_in_dim(values, (mine + d) % seqs_here, 0, keepdims=False)
            parts.append(hop(part, d))
        return jnp.concatenate(parts, axis=0)

    def from_sequence(values):
        parts = [values[:block_rows]]
        for d in range(1, seqs_here):
            parts.append(hop(values[d * block_rows : (d + 1) * block_rows], -d))
        stacked = jnp.stack(parts + parts)
        return lax.dynamic_slice_in_dim(stacked, (seqs_here - mine) % seqs_here, seqs_here, 0)

    groups = [[q * group + r for r in range(group)] for q in range(seqs_here)]
    swap = [(i, i ^ 1) for i in range(ctx)]

    def share_keys(k, v):
        if group == 2:
            other = lax.ppermute(jnp.stack([k, v]), "ctx", swap)
            return jnp.concatenate([k, other[0]]), jnp.concatenate([v, other[1]])
        both = lax.all_gather(jnp.stack([k, v]), "ctx", axis=1, tiled=True, axis_index_groups=groups)
        return both[0], both[1]

    def sum_keys(dk, dv):
        rows = dk.shape[0] // group
        if group == 2:
            other = lax.ppermute(jnp.stack([dk[rows:], dv[rows:]]), "ctx", swap)
            return (
                dk[:rows].astype(f32) + other[0].astype(f32),
                dv[:rows].astype(f32) + other[1].astype(f32),
            )
        both = lax.psum_scatter(
            jnp.stack([dk, dv]), "ctx", scatter_dimension=1, axis_index_groups=groups, tiled=True
        ).astype(f32)
        return both[0], both[1]

    def gather(shard):
        return lax.all_gather(shard, "seq", axis=0, tiled=True)

    def reduce_shard(grad):
        part = lax.psum_scatter(grad.astype(bf16), "seq", scatter_dimension=0, tiled=True)
        return lax.psum(part, "ctx").astype(f32)

    gain_one = gain_one.astype(f32)[:, None]
    gain_two = gain_two.astype(f32)[:, None]
    qkv_all = gather((w_qkv.astype(f32) * gain_one).astype(bf16))
    attn_all = gather(w_attn)
    in_all = gather((w_in.astype(f32) * gain_two).astype(bf16))
    mlp_all = gather(w_mlp)

    x = to_sequence(tokens).astype(f32)
    g = to_sequence(cotangent)

    came_from = (mine - jnp.arange(seqs_here, dtype=jnp.int32)) % seqs_here
    starts = (came_from * group + place) * block_rows
    positions = (starts[:, None] + jnp.arange(block_rows, dtype=jnp.int32)).reshape(-1)
    frequency = rope_base ** (-(jnp.arange(HD // 2, dtype=f32) * 2.0) / HD)
    angles = positions.astype(f32)[:, None] * frequency[None, :]
    cosines = jnp.tile(jnp.cos(angles), (1, 2 * H))
    sines = jnp.tile(jnp.sin(angles), (1, 2 * H))

    xhat, scale_one = normalize(x)
    h1 = xhat.astype(bf16)
    qkv = dot(h1, qkv_all, NN)
    q = rotate(qkv[:, :width], cosines, sines).astype(bf16)
    k = rotate(qkv[:, width : 2 * width], cosines, sines).astype(bf16)
    v = qkv[:, 2 * width :].astype(bf16)
    keys, values = share_keys(k, v)
    attn, lse = attend(q, keys, values)
    x2 = x + dot(attn, attn_all, NN)
    xhat2, scale_two = normalize(x2)
    h2 = xhat2.astype(bf16)
    gu = dot(h2, in_all, NN)
    gate, up = gu[:, :FF], gu[:, FF:]
    cumulative = 0.5 * (1.0 + lax.erf(gate * (0.5**0.5)))
    gelu = gate * cumulative
    slope = cumulative + gate * jnp.exp(-0.5 * gate * gate) * 0.3989422804014327
    a = (gelu * up).astype(bf16)
    layer_output = from_sequence((x2 + dot(a, mlp_all, NN)).astype(bf16))
    grad_mlp = reduce_shard(dot(a, g, TN))
    da = dot(g, mlp_all, NT)
    dgu = jnp.concatenate([da * up * slope, da * gelu], axis=-1).astype(bf16)
    raw_in = reduce_shard(dot(h2, dgu, TN))
    dx2 = g.astype(f32) + norm_back(dot(dgu, in_all, NT), xhat2, scale_two)
    dy = dx2.astype(bf16)
    grad_attn = reduce_shard(dot(attn, dy, TN))
    do = dot(dy, attn_all, NT).astype(bf16)
    dq, dk, dv = attend_back(q, keys, values, do, lse)
    dk, dv = sum_keys(dk, dv)
    dqkv = jnp.concatenate(
        [unrotate(dq, cosines, sines), unrotate(dk, cosines, sines), dv], axis=-1
    ).astype(bf16)
    raw_qkv = reduce_shard(dot(h1, dqkv, TN))
    dx = dx2 + norm_back(dot(dqkv, qkv_all, NT), xhat, scale_one)
    grad_tokens = from_sequence(dx.astype(bf16)).astype(f32)
    return (
        layer_output,
        grad_tokens,
        raw_qkv * gain_one,
        grad_attn,
        raw_in * gain_two,
        grad_mlp,
        jnp.sum(raw_qkv * w_qkv.astype(f32), axis=-1),
        jnp.sum(raw_in * w_in.astype(f32), axis=-1),
    )


def solution(mesh):
    split = P("seq", "ctx", None)
    rows = P("seq", None)

    def whole(tokens, *others):
        seqs_here = tokens.shape[0] // mesh.shape["seq"]
        group = mesh.shape["ctx"] // seqs_here
        return jax.shard_map(
            functools.partial(body, seqs_here, group),
            mesh=mesh,
            in_specs=(split, rows, rows, rows, rows, P("seq"), P("seq"), split),
            out_specs=(split, split, rows, rows, rows, rows, P("seq"), P("seq")),
            check_vma=False,
        )(tokens, *others)

    return whole
```

time: 862 us -> 437 us (0.51)
  waiting for transfers between devices: 486 us -> 286 us
  matrix products: 131 us -> 42.5 us
  local copies, waits for them, and re-layouts: 94.2 us -> 18.7 us
  other arithmetic: 87.4 us -> 26.4 us
  blocking collectives: 36.7 us -> 0 us
  Pallas kernels: 0 us -> 25.8 us
  starting transfers between devices: 2.89 us -> 22.5 us
    ppermute x15 -> x14, waiting for transfers between devices: 212 us -> 29.4 us  [the longest x12 26.5 us: hop(): return lax.ppermute(block, 'ctx', route)]
    all_gather x6 -> x4, waiting for transfers between devices: 199 us -> 102 us  [gather(): return lax.all_gather(shard, 'seq', axis=0, tiled=True)]
    dot_general x54 -> x12, matrix products: 131 us -> 42.5 us  [dot(): return lax.dot_general(a, b, (dims, ((), ())), preferred_element_type=f32)]
    convert_element_type x27 -> x10, other arithmetic: 68 us -> 11.8 us  [the longest x2 3.88 us: reduce_shard(): return lax.psum(part, 'ctx').astype(f32)]
    reduce_scatter x4, waiting for transfers between devices: 39.9 us -> 84 us  [reduce_shard(): lax.psum_scatter(grad.astype(bf16), 'seq', scatter_dimension=0, tiled=True)]
    psum x1, waiting for transfers between devices: 33.2 us -> 70 us  [reduce_shard(): return lax.psum(part, 'ctx').astype(f32)]
    slice x28 -> x9, local copies, waits for them, and re-layouts: 29.7 us -> 3.28 us  [the longest x3 1.5 us: turn(): values[:, :-(HD // 2)]]
    pallas_call x0 -> x2, Pallas kernels: none -> 25.8 us  [the longest x1 15.9 us: attend_back(): pl.pallas_call(attend_back_kernel, grid=(width // PAIR,), in_specs=[colum...]
  transfers between devices with their start and end apart: 26 -> 23, of which waited for: 23 -> 15; matrix products, arithmetic and copies ran while one was open for 31% -> 13% of each run, Pallas kernels for 0% -> 6%
where the time goes in v1:
time: 437 us
  waiting for transfers between devices  286 us (65%)
  matrix products  42.5 us (10%)
  other arithmetic  26.4 us (6%)
  Pallas kernels  25.8 us (6%)
  starting transfers between devices  22.5 us (5%)
  local copies, waits for them, and re-layouts  18.7 us (4%)
  between operations  14.6 us (3%)
    all_gather x4, waiting for transfers between devices, gather(): return lax.all_gather(shard, 'seq', axis=0, tiled=True)  102 us
    reduce_scatter x4, waiting for transfers between devices, reduce_shard(): lax.psum_scatter(grad.astype(bf16), 'seq', scatter_dimension=0, tiled=True)  84 us
    psum x1, waiting for transfers between devices, reduce_shard(): return lax.psum(part, 'ctx').astype(f32)  70 us
    dot_general x12, matrix products, dot(): return lax.dot_general(a, b, (dims, ((), ())), preferred_element_type=f32)  42.5 us
    ppermute x12, waiting for transfers between devices, hop(): return lax.ppermute(block, 'ctx', route)  26.5 us
    ppermute x12, starting transfers between devices, hop(): return lax.ppermute(block, 'ctx', route)  21.8 us
    pallas_call x1, Pallas kernels, attend_back(): pl.pallas_call(attend_back_kernel, grid=(width // PAIR,), in_specs=[colum...  15.9 us
    pallas_call x1, Pallas kernels, attend(): pl.pallas_call(attend_kernel, grid=(width // PAIR,), in_specs=[column_blo...  9.88 us
  transfers between devices with their start and end apart: 23, of which 15 were waited for; matrix products, arithmetic and copies ran while one was open for 13% of the time, Pallas kernels for 6%

profile of v1, /device:TPU:0, one launch (start us, length us, event | category | flops | bytes accessed | tf_op | source)
XLA Modules:
  0.0 436.6 jit_solution(1491221120941749706)
XLA Ops:
  8.4 2.4 fusion
  14.3 3.0 collective-permute-start
  17.4 2.0 collective-permute-start.2
  26.2 6.9 %collective-permute-done.1 = bf16[96,768]{1,0:T(8,128)(2,1)} collective-permute-done((bf16[96,768]{1,0:T(8,128)(2,1)}, bf16[96,768]{1,0:T(8,128)(2,1)}, u32[]{:S(2)}, u32[]{:S(2)}) %collective-permute-start.1) | collective-permute-done | bytes 147488 | tf_op jit(solution)/shard_map/ppermute | solution.py:152
  35.8 25.2 %all-gather.5.cloned.1.call-done = bf16[768,2304]{1,0:T(8,128)(2,1)} async-done(((bf16[192,2304]{1,0:T(8,128)(2,1)}), bf16[768,2304]{1,0:T(8,128)(2,1)}) %all-gather.5.cloned.1.call-update) | async-done | bytes 3538960 | tf_op jit(solution)/shard_map/all_gather | solution.py:192
  60.9 3.8 fusion.60
  69.0 2.0 dynamic-slice_bitcast_fusion.3
  72.5 2.3 collective-permute-start.9
  78.4 9.9 %shard_map.143 = (bf16[384,768]{1,0:T(8,128)(2,1)S(1)}, f32[384,768]{1,0:T(8,128)S(1)}) custom-call(bf16[384,768]{1,0:T(8,128)(2,1)S(1)} %get-tuple-element.27.q_ref, bf16[768,768]{1,0:T(8,128)(2,1)S(1)} %pad_maximum_fusion.3.k_ref, bf16[768,768]{1,0:T(8,128)(2,1)} %pad_maximum_fusion.4.v_ref), custom_call_target="tpu_custom_call" | custom-call | flops 905969664 | bytes 7077888 | tf_op jit(solution)/shard_map/pallas_call | solution.py:69
  90.5 2.1 fusion.77
  93.6 46.6 %all-gather.9.cloned.1.call-done = bf16[768,2304]{1,0:T(8,128)(2,1)} async-done(((bf16[192,2304]{1,0:T(8,128)(2,1)}), bf16[768,2304]{1,0:T(8,128)(2,1)}) %all-gather.9.cloned.1.call-update) | async-done | bytes 3538960 | tf_op jit(solution)/shard_map/all_gather | solution.py:192
  140.2 5.5 %fusion.64 = f32[384,2304]{1,0:T(8,128)} fusion(bf16[768,2304]{1,0:T(8,128)(2,1)} %all-gather.9.cloned.1.call-done, f32[384,768]{1,0:T(8,128)S(1)} %get-tuple-element.75, f32[384]{0:T(512)} %add_rsqrt_fusion, f32[384]{0:T(512)S(1)} %broadcast_multiply_fusion.4), kind=kOutput, calls=%fused_computation.149 | convolution fusion | flops 1359839232 | bytes 8260608 | tf_op jit(solution)/shard_map/dot_general | solution.py:22
  145.7 28.8 %all-gather.11.cloned.1.call-done = bf16[1152,768]{1,0:T(8,128)(2,1)} async-done(((bf16[288,768]{1,0:T(8,128)(2,1)}), bf16[1152,768]{1,0:T(8,128)(2,1)}) %all-gather.11.cloned.1.call-update) | async-done | bytes 1769488 | tf_op jit(solution)/shard_map/all_gather | solution.py:192
  174.6 5.1 %fusion.9 = (bf16[384,1152]{1,0:T(8,128)(2,1)S(1)}, bf16[384,1152]{1,0:T(8,128)(2,1)S(1)}, bf16[384,1152]{1,0:T(8,128)(2,1)}) fusion(f32[384,2304]{1,0:T(8,128)} %fusion.64, bf16[1152,768]{1,0:T(8,128)(2,1)} %all-gather.11.cloned.1.call-done, bf16[96,768]{1,0:T(8,128)(2,1)} %collective-permute-done.9, bf16[96,768]{1,0:T(8,128)(2,1)} %collective-permute-done.8, ...), kind=kOutput, calls=%fused_computation.19 | convolution fusion | flops 688914432 | bytes 8552448 | tf_op jit(solution)/shard_map/dot_general | solution.py:22
  186.1 3.6 convolution_convert_fusion.2
  190.3 5.9 %convolution_convert_fusion = bf16[768,2304]{1,0:T(8,128)(2,1)} fusion(bf16[384,1152]{1,0:T(8,128)(2,1)} %copy-done.36, bf16[384,1152]{1,0:T(8,128)(2,1)} %copy-done.35, f32[384,768]{1,0:T(8,128)} %copy-done.5, f32[384]{0:T(512)S(1)} %copy-done.25, f32[384]{0:T(512)S(1)} %broadcast_multiply_fusion.4), kind=kOutput, calls=%fused_computation | convolution fusion | flops 1365147648 | bytes 6491136 | tf_op jit(solution)/shard_map/dot_general | solution.py:22
  198.5 15.9 %shard_map.144 = (f32[384,768]{1,0:T(8,128)S(1)}, bf16[768,768]{1,0:T(8,128)(2,1)S(1)}, bf16[768,768]{1,0:T(8,128)(2,1)}) custom-call(bf16[384,768]{1,0:T(8,128)(2,1)S(1)} %get-tuple-element.27.q_ref, bf16[768,768]{1,0:T(8,128)(2,1)} %copy-done, bf16[768,768]{1,0:T(8,128)(2,1)} %pad_maximum_fusion.4.v_ref, ...), custom_call_target="tpu_custom_call" | custom-call | flops 2264924160 | bytes 10616832 | tf_op jit(solution)/shard_map/pallas_call | solution.py:90
  215.8 2.8 collective-permute-done.10
  222.9 5.2 %convolution_convert_fusion.1 = bf16[768,2304]{1,0:T(8,128)(2,1)} fusion(bf16[384,768]{1,0:T(8,128)(2,1)S(1)} %get-tuple-element.41, bf16[384,768]{1,0:T(8,128)(2,1)S(1)} %get-tuple-element.40, bf16[384,768]{1,0:T(8,128)(2,1)S(1)} %get-tuple-element.39, f32[384]{0:T(512)S(1)} %copy-done.23, f32[384]{0:T(512)S(1)} %broadcast_multiply_fusion.5, ...), kind=kOutput, calls=%fused_computation.1 | convolution fusion | flops 1369276416 | bytes 5901312 | tf_op jit(solution)/shard_map/dot_general | solution.py:22
  229.4 2.9 fusion.15
  233.7 2.4 collective-permute-start.5
  237.6 6.5 %collective-permute-done.4 = bf16[96,768]{1,0:T(8,128)(2,1)S(1)} collective-permute-done((bf16[96,768]{1,0:T(8,128)(2,1)S(1)}, bf16[96,768]{1,0:T(8,128)(2,1)S(1)}, u32[]{:S(2)}, u32[]{:S(2)}) %collective-permute-start.4) | collective-permute-done | bytes 147488 | tf_op jit(solution)/shard_map/ppermute | solution.py:152
  244.1 2.3 collective-permute-done.5
  248.0 2.8 fusion.66
  252.3 3.7 collective-permute-start.13
  258.5 7.3 %collective-permute-done.11 = bf16[96,768]{1,0:T(8,128)(2,1)S(1)} collective-permute-done((bf16[96,768]{1,0:T(8,128)(2,1)S(1)}, bf16[96,768]{1,0:T(8,128)(2,1)S(1)}, u32[]{:S(2)}, u32[]{:S(2)}) %collective-permute-start.11) | collective-permute-done | bytes 147488 | tf_op jit(solution)/shard_map/ppermute | solution.py:152
  266.5 33.6 %reduce-scatter.9.cloned.1.call-done = bf16[192,2304]{1,0:T(8,128)(2,1)} async-done(((bf16[768,2304]{1,0:T(8,128)(2,1)}), bf16[192,2304]{1,0:T(8,128)(2,1)}) %reduce-scatter.9.cloned.1.call-update) | async-done | bytes 884752 | tf_op jit(solution)/shard_map/reduce_scatter | solution.py:195
  300.2 50.3 %reduce-scatter.5.cloned.1.call-done = bf16[192,2304]{1,0:T(8,128)(2,1)} async-done(((bf16[768,2304]{1,0:T(8,128)(2,1)}), bf16[192,2304]{1,0:T(8,128)(2,1)}) %reduce-scatter.5.cloned.1.call-update) | async-done | bytes 884752 | tf_op jit(solution)/shard_map/reduce_scatter | solution.py:195
  351.8 70.0 %all-reduce.3.cloned.1.call-done = (bf16[192,2304]{1,0:T(8,128)(2,1)}, bf16[192,768]{1,0:T(8,128)(2,1)}, bf16[192,2304]{1,0:T(8,128)(2,1)}, bf16[288,768]{1,0:T(8,128)(2,1)}) async-done(((bf16[192,2304]{1,0:T(8,128)(2,1)}, bf16[192,768]{1,0:T(8,128)(2,1)}, bf16[192,2304]{1,0:T(8,128)(2,1)}, bf16[288,768]{1,0:T(8,128)(2,1)}), (bf16[192,2304]{1,0:T(8,128)(2,1)}, bf16[192,768]{1,0:T(8,128)(2,1)}, ...) | async-done | bytes 2506768 | tf_op jit(solution)/shard_map/psum | solution.py:196
  423.7 2.0 convert_element_type.144
  425.7 2.2 fusion.2
  427.9 2.2 fusion.3
  (183 shorter events, 54.5 us)
Async XLA Ops:
  7.2 53.8 %all-gather.5.cloned.1.call-start = ((), (), s32[]{:S(2)}) async-start(), calls=%async_computation.4 | async-start | bytes 4423680 | tf_op jit(solution)/shard_map/all_gather | solution.py:192
  10.8 79.7 %all-gather.7.cloned.1.call-start = ((), (), s32[]{:S(2)}) async-start(), calls=%async_computation.5 | async-start | bytes 1474560 | tf_op jit(solution)/shard_map/all_gather | solution.py:192
  11.6 128.7 %all-gather.9.cloned.1.call-start = ((), (), s32[]{:S(2)}) async-start(), calls=%async_computation.6 | async-start | bytes 4423680 | tf_op jit(solution)/shard_map/all_gather | solution.py:192
  13.4 161.2 %all-gather.11.cloned.1.call-start = ((), (), s32[]{:S(2)}) async-start(), calls=%async_computation.7 | async-start | bytes 2211840 | tf_op jit(solution)/shard_map/all_gather | solution.py:192
  14.3 10.1 %collective-permute-start = (bf16[96,768]{1,0:T(8,128)(2,1)}, bf16[96,768]{1,0:T(8,128)(2,1)}, u32[]{:S(2)}, u32[]{:S(2)}) collective-permute-start(bf16[96,768]{1,0:T(8,128)(2,1)} %get-tuple-element.69), channel_id=1, source_target_pairs={{0,2},{1,3},{2,4},{3,5},{4,6},{5,7},{6,0},{7,1},{8,10},{9,11},{10,... | collective-permute-start | bytes 442376 | tf_op jit(solution)/shard_map/ppermute | solution.py:152
  17.4 8.8 %collective-permute-start.2 = (bf16[96,768]{1,0:T(8,128)(2,1)}, bf16[96,768]{1,0:T(8,128)(2,1)}, u32[]{:S(2)}, u32[]{:S(2)}) collective-permute-start(bf16[96,768]{1,0:T(8,128)(2,1)} %get-tuple-element.70), channel_id=1, source_target_pairs={{0,6},{1,7},{2,0},{3,1},{4,2},{5,3},{6,4},{7,5},{8,14},{9,15},{10,... | collective-permute-start | bytes 442376 | tf_op jit(solution)/shard_map/ppermute | solution.py:152
  19.4 13.6 %collective-permute-start.1 = (bf16[96,768]{1,0:T(8,128)(2,1)}, bf16[96,768]{1,0:T(8,128)(2,1)}, u32[]{:S(2)}, u32[]{:S(2)}) collective-permute-start(bf16[96,768]{1,0:T(8,128)(2,1)} %get-tuple-element.71), channel_id=1, source_target_pairs={{0,4},{1,5},{2,6},{3,7},{4,0},{5,1},{6,2},{7,3},{8,12},{9,13},{10,... | collective-permute-start | bytes 442376 | tf_op jit(solution)/shard_map/ppermute | solution.py:152
  21.5 44.3 %copy-start.30 = (pred[768]{0:T(1024)(128)(4,1)}, pred[768]{0:T(1024)(128)(4,1)S(1)}, u32[]{:S(2)}) copy-start(pred[768]{0:T(1024)(128)(4,1)S(1)} %fusion.50) | copy-start | bytes 2308
  22.0 43.8 %copy-start.3 = (f32[384,768]{1,0:T(8,128)}, f32[384,768]{1,0:T(8,128)S(1)}, u32[]{:S(2)}) copy-start(f32[384,768]{1,0:T(8,128)S(1)} %copy.17) | copy-start | bytes 3538948
  23.4 37.6 %copy-start.10 = (bf16[96,768]{1,0:T(8,128)(2,1)S(1)}, bf16[96,768]{1,0:T(8,128)(2,1)}, u32[]{:S(2)}) copy-start(bf16[96,768]{1,0:T(8,128)(2,1)} %get-tuple-element.68) | copy-start | bytes 442372
  35.8 29.0 %copy-start.22 = (f32[384]{0:T(512)}, f32[384]{0:T(512)S(1)}, u32[]{:S(2)}) copy-start(f32[384]{0:T(512)S(1)} %add_rsqrt_fusion.1) | copy-start | bytes 4612
  68.9 7.8 %collective-permute-start.3 = (bf16[2,384,768]{2,1,0:T(8,128)(2,1)}, bf16[2,384,768]{2,1,0:T(8,128)(2,1)S(1)}, u32[]{:S(2)}, u32[]{:S(2)}) collective-permute-start(bf16[2,384,768]{2,1,0:T(8,128)(2,1)} %pad_maximum_fusion.2), channel_id=1, source_target_pairs={{0,1},{1,0},{2,3},{3,2},{4,5},{5,4},{6,7},{7,6},{8,9},{9,8},{10,11... | collective-permute-start | bytes 3538952 | tf_op jit(solution)/shard_map/ppermute | solution.py:173
  69.0 197.6 %reduce-scatter.7.cloned.1.call-start = ((), (), s32[]{:S(2)}) async-start(), calls=%async_computation.9 | async-start | bytes 1474560 | tf_op jit(solution)/shard_map/reduce_scatter | solution.py:195
  71.0 74.7 %collective-permute-start.7 = (bf16[96,768]{1,0:T(8,128)(2,1)}, bf16[96,768]{1,0:T(8,128)(2,1)}, u32[]{:S(2)}, u32[]{:S(2)}) collective-permute-start(bf16[96,768]{1,0:T(8,128)(2,1)} %get-tuple-element.62), channel_id=1, source_target_pairs={{0,2},{1,3},{2,4},{3,5},{4,6},{5,7},{6,0},{7,1},{8,10},{9,11},{10,... | collective-permute-start | bytes 442376 | tf_op jit(solution)/shard_map/ppermute | solution.py:152
  72.5 73.3 %collective-permute-start.9 = (bf16[96,768]{1,0:T(8,128)(2,1)}, bf16[96,768]{1,0:T(8,128)(2,1)}, u32[]{:S(2)}, u32[]{:S(2)}) collective-permute-start(bf16[96,768]{1,0:T(8,128)(2,1)} %get-tuple-element.63), channel_id=1, source_target_pairs={{0,6},{1,7},{2,0},{3,1},{4,2},{5,3},{6,4},{7,5},{8,14},{9,15},{10,... | collective-permute-start | bytes 442376 | tf_op jit(solution)/shard_map/ppermute | solution.py:152
  74.8 70.9 %collective-permute-start.8 = (bf16[96,768]{1,0:T(8,128)(2,1)}, bf16[96,768]{1,0:T(8,128)(2,1)}, u32[]{:S(2)}, u32[]{:S(2)}) collective-permute-start(bf16[96,768]{1,0:T(8,128)(2,1)} %get-tuple-element.64), channel_id=1, source_target_pairs={{0,4},{1,5},{2,6},{3,7},{4,0},{5,1},{6,2},{7,3},{8,12},{9,13},{10,... | collective-permute-start | bytes 442376 | tf_op jit(solution)/shard_map/ppermute | solution.py:152
  92.6 87.1 %copy-start.5 = (f32[384,768]{1,0:T(8,128)}, f32[384,768]{1,0:T(8,128)S(1)}, u32[]{:S(2)}) copy-start(f32[384,768]{1,0:T(8,128)S(1)} %get-tuple-element.75) | copy-start | bytes 3538948
  174.6 5.2 %copy-start.33 = (bf16[768,2304]{1,0:T(8,128)(2,1)S(1)}, bf16[768,2304]{1,0:T(8,128)(2,1)}, u32[]{:S(2)}) copy-start(bf16[768,2304]{1,0:T(8,128)(2,1)} %all-gather.9.cloned.1.call-done) | copy-start | bytes 10616836
  185.2 81.4 %reduce-scatter.11.cloned.1.call-start = ((), (), s32[]{:S(2)}) async-start(), calls=%async_computation.11 | async-start | bytes 2211840 | tf_op jit(solution)/shard_map/reduce_scatter | solution.py:195
  189.7 110.5 %reduce-scatter.9.cloned.1.call-start = ((), (), s32[]{:S(2)}) async-start(), calls=%async_computation.10 | async-start | bytes 4423680 | tf_op jit(solution)/shard_map/reduce_scatter | solution.py:195
  196.2 154.3 %reduce-scatter.5.cloned.1.call-start = ((), (), s32[]{:S(2)}) async-start(), calls=%async_computation.8 | async-start | bytes 4423680 | tf_op jit(solution)/shard_map/reduce_scatter | solution.py:195
  215.7 2.9 collective-permute-start.10
  228.1 193.6 %all-reduce.3.cloned.1.call-start = ((), (), s32[]{:S(2)}) async-start(), calls=%async_computation.12 | async-start | bytes 5013504 | tf_op jit(solution)/shard_map/psum | solution.py:196
  229.4 18.0 %copy-start.32 = (bf16[768,2304]{1,0:T(8,128)(2,1)S(1)}, bf16[768,2304]{1,0:T(8,128)(2,1)}, u32[]{:S(2)}) copy-start(bf16[768,2304]{1,0:T(8,128)(2,1)} %all-gather.5.cloned.1.call-done) | copy-start | bytes 10616836
  232.4 14.1 %collective-permute-start.6 = (bf16[96,768]{1,0:T(8,128)(2,1)S(1)}, bf16[96,768]{1,0:T(8,128)(2,1)S(1)}, u32[]{:S(2)}, u32[]{:S(2)}) collective-permute-start(bf16[96,768]{1,0:T(8,128)(2,1)S(1)} %get-tuple-element.65), channel_id=1, source_target_pairs={{0,2},{1,3},{2,4},{3,5},{4,6},{5,7},{6,0},{7,1},{8,10},{9,11},{10,... | collective-permute-start | bytes 442376 | tf_op jit(solution)/shard_map/ppermute | solution.py:152
  233.7 12.7 %collective-permute-start.5 = (bf16[96,768]{1,0:T(8,128)(2,1)S(1)}, bf16[96,768]{1,0:T(8,128)(2,1)S(1)}, u32[]{:S(2)}, u32[]{:S(2)}) collective-permute-start(bf16[96,768]{1,0:T(8,128)(2,1)S(1)} %get-tuple-element.66), channel_id=1, source_target_pairs={{0,4},{1,5},{2,6},{3,7},{4,0},{5,1},{6,2},{7,3},{8,12},{9,13},{10,... | collective-permute-start | bytes 442376 | tf_op jit(solution)/shard_map/ppermute | solution.py:152
  236.1 8.0 %collective-permute-start.4 = (bf16[96,768]{1,0:T(8,128)(2,1)S(1)}, bf16[96,768]{1,0:T(8,128)(2,1)S(1)}, u32[]{:S(2)}, u32[]{:S(2)}) collective-permute-start(bf16[96,768]{1,0:T(8,128)(2,1)S(1)} %get-tuple-element.67), channel_id=1, source_target_pairs={{0,6},{1,7},{2,0},{3,1},{4,2},{5,3},{6,4},{7,5},{8,14},{9,15},{10,... | collective-permute-start | bytes 442376 | tf_op jit(solution)/shard_map/ppermute | solution.py:152
  252.3 98.2 %collective-permute-start.13 = (bf16[96,768]{1,0:T(8,128)(2,1)S(1)}, bf16[96,768]{1,0:T(8,128)(2,1)S(1)}, u32[]{:S(2)}, u32[]{:S(2)}) collective-permute-start(bf16[96,768]{1,0:T(8,128)(2,1)S(1)} %get-tuple-element.58), channel_id=1, source_target_pairs={{0,2},{1,3},{2,4},{3,5},{4,6},{5,7},{6,0},{7,1},{8,10},{9,11},{10,... | collective-permute-start | bytes 442376 | tf_op jit(solution)/shard_map/ppermute | solution.py:152
  256.0 10.5 %collective-permute-start.12 = (bf16[96,768]{1,0:T(8,128)(2,1)S(1)}, bf16[96,768]{1,0:T(8,128)(2,1)S(1)}, u32[]{:S(2)}, u32[]{:S(2)}) collective-permute-start(bf16[96,768]{1,0:T(8,128)(2,1)S(1)} %get-tuple-element.59), channel_id=1, source_target_pairs={{0,4},{1,5},{2,6},{3,7},{4,0},{5,1},{6,2},{7,3},{8,12},{9,13},{10,... | collective-permute-start | bytes 442376 | tf_op jit(solution)/shard_map/ppermute | solution.py:152
  257.3 8.4 %collective-permute-start.11 = (bf16[96,768]{1,0:T(8,128)(2,1)S(1)}, bf16[96,768]{1,0:T(8,128)(2,1)S(1)}, u32[]{:S(2)}, u32[]{:S(2)}) collective-permute-start(bf16[96,768]{1,0:T(8,128)(2,1)S(1)} %get-tuple-element.60), channel_id=1, source_target_pairs={{0,6},{1,7},{2,0},{3,1},{4,2},{5,3},{6,4},{7,5},{8,14},{9,15},{10,... | collective-permute-start | bytes 442376 | tf_op jit(solution)/shard_map/ppermute | solution.py:152
  351.7 73.9 %copy-start.7 = (bf16[192,2304]{1,0:T(8,128)(2,1)S(1)}, bf16[192,2304]{1,0:T(8,128)(2,1)}, u32[]{:S(2)}) copy-start(bf16[192,2304]{1,0:T(8,128)(2,1)} %param.9) | copy-start | bytes 2654212
  351.8 73.9 %copy-start.27 = (f32[192]{0:T(256)S(1)}, f32[192]{0:T(256)}, u32[]{:S(2)}) copy-start(f32[192]{0:T(256)} %copy-done.26) | copy-start | bytes 2308
  (28 other events, 52.0 us)
Sparse Core Ops, SparseCore 0:
  11.0 49.9 all-gather.4
  62.8 27.7 all-gather.6
  93.0 47.2 all-gather.8
  141.9 32.5 all-gather.10
  185.3 28.5 reduce-scatter.6
  217.3 32.4 reduce-scatter.10
  252.9 47.2 reduce-scatter.8
  303.2 47.2 reduce-scatter.4
  353.2 68.5 all-reduce.2

commit v2 on v1

--- a/solution.py
+++ b/solution.py
@@ -188,16 +188,40 @@
         ).astype(f32)
         return both[0], both[1]
 
+    core = me % 2
+    parity = [[i for i in range(ctx) if i % 2 == r] for r in range(2)]
+
+    def half_of(values, which):
+        half = values.shape[1] // 2
+        return lax.dynamic_slice_in_dim(values, which * half, half, 1)
+
+    def join(own, other):
+        left = jnp.where(core == 0, own, other)
+        right = jnp.where(core == 0, other, own)
+        return jnp.concatenate([left, right], axis=1)
+
     def gather(shard):
-        return lax.all_gather(shard, "seq", axis=0, tiled=True)
-
-    def reduce_shard(grad):
-        part = lax.psum_scatter(grad.astype(bf16), "seq", scatter_dimension=0, tiled=True)
-        return lax.psum(part, "ctx").astype(f32)
+        return lax.all_gather(half_of(shard, core), "seq", axis=0, tiled=True)
+
+    def both_halves(own):
+        return join(own, lax.ppermute(own, "ctx", swap))
+
+    def reduce_pair(left, right):
+        sent = dot(left, half_of(right, 1 - core), TN).astype(bf16)
+        got = lax.ppermute(sent, "ctx", swap)
+        kept = dot(left, half_of(right, core), TN) + got.astype(f32)
+        return kept.astype(bf16)
+
+    def scatter(kept):
+        return lax.psum_scatter(kept, "seq", scatter_dimension=0, tiled=True)
+
+    def reduce_ctx(parts):
+        totals = lax.psum(parts, "ctx", axis_index_groups=parity)
+        return [join(t, lax.ppermute(t, "ctx", swap)).astype(f32) for t in totals]
 
     gain_one = gain_one.astype(f32)[:, None]
     gain_two = gain_two.astype(f32)[:, None]
-    qkv_all = gather((w_qkv.astype(f32) * gain_one).astype(bf16))
+    qkv_all = both_halves(gather((w_qkv.astype(f32) * gain_one).astype(bf16)))
     attn_all = gather(w_attn)
     in_all = gather((w_in.astype(f32) * gain_two).astype(bf16))
     mlp_all = gather(w_mlp)
@@ -220,7 +244,10 @@
     k = rotate(qkv[:, width : 2 * width], cosines, sines).astype(bf16)
     v = qkv[:, 2 * width :].astype(bf16)
     keys, values = share_keys(k, v)
+    attn_all = both_halves(attn_all)
     attn, lse = attend(q, keys, values)
+    attn, in_all, mlp_all = lax.optimization_barrier((attn, in_all, mlp_all))
+    in_all, mlp_all = both_halves(in_all), both_halves(mlp_all)
     x2 = x + dot(attn, attn_all, NN)
     xhat2, scale_two = normalize(x2)
     h2 = xhat2.astype(bf16)
@@ -231,20 +258,27 @@
     slope = cumulative + gate * jnp.exp(-0.5 * gate * gate) * 0.3989422804014327
     a = (gelu * up).astype(bf16)
     layer_output = from_sequence((x2 + dot(a, mlp_all, NN)).astype(bf16))
-    grad_mlp = reduce_shard(dot(a, g, TN))
+    part_mlp = reduce_pair(a, g)
     da = dot(g, mlp_all, NT)
     dgu = jnp.concatenate([da * up * slope, da * gelu], axis=-1).astype(bf16)
-    raw_in = reduce_shard(dot(h2, dgu, TN))
+    part_in = reduce_pair(h2, dgu)
     dx2 = g.astype(f32) + norm_back(dot(dgu, in_all, NT), xhat2, scale_two)
     dy = dx2.astype(bf16)
-    grad_attn = reduce_shard(dot(attn, dy, TN))
+    part_attn = reduce_pair(attn, dy)
     do = dot(dy, attn_all, NT).astype(bf16)
+    do, part_mlp, part_in, part_attn = lax.optimization_barrier((do, part_mlp, part_in, part_attn))
+    parts = [scatter(part_mlp), scatter(part_in), scatter(part_attn)]
+    grad_mlp, raw_in, grad_attn = reduce_ctx(parts)
     dq, dk, dv = attend_back(q, keys, values, do, lse)
     dk, dv = sum_keys(dk, dv)
     dqkv = jnp.concatenate(
         [unrotate(dq, cosines, sines), unrotate(dk, cosines, sines), dv], axis=-1
     ).astype(bf16)
-    raw_qkv = reduce_shard(dot(h1, dqkv, TN))
+    part_qkv = scatter(reduce_pair(h1, dqkv))
+    part_qkv, grad_mlp, raw_in, grad_attn = lax.optimization_barrier(
+        (part_qkv, grad_mlp, raw_in, grad_attn)
+    )
+    (raw_qkv,) = reduce_ctx([part_qkv])
     dx = dx2 + norm_back(dot(dqkv, qkv_all, NT), xhat, scale_one)
     grad_tokens = from_sequence(dx.astype(bf16)).astype(f32)
     return (

time: 437 us -> 387 us (0.89)
  waiting for transfers between devices: 286 us -> 184 us
  blocking collectives: 0 us -> 28.7 us
  other arithmetic: 26.4 us -> 38.3 us
  local copies, waits for them, and re-layouts: 18.7 us -> 29.3 us
    all_gather x4 -> x2, waiting for transfers between devices: 102 us -> 26.4 us  [gather(): return lax.all_gather(half_of(shard, core), 'seq', axis=0, tiled=True)]
    all_gather x0 -> x2, blocking collectives: none -> 28.7 us  [gather(): return lax.all_gather(half_of(shard, core), 'seq', axis=0, tiled=True)]
    reduce_scatter x4, waiting for transfers between devices: 84 us -> 62.6 us  [scatter(): return lax.psum_scatter(kept, 'seq', scatter_dimension=0, tiled=True)]
    psum x1 -> x2, waiting for transfers between devices: 70 us -> 59.6 us  [reduce_ctx(): totals = lax.psum(parts, 'ctx', axis_index_groups=parity)]
    select_n x0 -> x8, other arithmetic: none -> 7.25 us  [join(): left = jnp.where(core == 0, own, other)]
    unnamed x88 -> x136, local copies, waits for them, and re-layouts: 8.56 us -> 15.2 us
    ppermute x12, waiting for transfers between devices: 26.5 us -> 32.3 us  [hop(): return lax.ppermute(block, 'ctx', route)]
    dot_general x12 -> x16, matrix products: 42.5 us -> 42 us  [dot(): return lax.dot_general(a, b, (dims, ((), ())), preferred_element_type=f32)]
  transfers between devices with their start and end apart: 23 -> 34, of which waited for: 15 -> 12; matrix products, arithmetic and copies ran while one was open for 13% -> 22% of each run, Pallas kernels for 6% -> 7%
where the time goes in v2:
time: 387 us; the launch traced here: 386 us
  waiting for transfers between devices  184 us (48%)
  matrix products  42 us (11%)
  other arithmetic  38.3 us (10%)
  local copies, waits for them, and re-layouts  29.3 us (8%)
  blocking collectives  28.7 us (7%)
  Pallas kernels  26.1 us (7%)
  starting transfers between devices  22.4 us (6%)
  between operations  15.2 us (4%)
    reduce_scatter x4, waiting for transfers between devices, scatter(): return lax.psum_scatter(kept, 'seq', scatter_dimension=0, tiled=True)  62.6 us
    psum x2, waiting for transfers between devices, reduce_ctx(): totals = lax.psum(parts, 'ctx', axis_index_groups=parity)  59.6 us
    dot_general x16, matrix products, dot(): return lax.dot_general(a, b, (dims, ((), ())), preferred_element_type=f32)  42 us
    ppermute x12, waiting for transfers between devices, hop(): return lax.ppermute(block, 'ctx', route)  32.3 us
    all_gather x2, blocking collectives, gather(): return lax.all_gather(half_of(shard, core), 'seq', axis=0, tiled=True)  28.7 us
    all_gather x2, waiting for transfers between devices, gather(): return lax.all_gather(half_of(shard, core), 'seq', axis=0, tiled=True)  26.4 us
    ppermute x12, starting transfers between devices, hop(): return lax.ppermute(block, 'ctx', route)  19.4 us
    pallas_call x1, Pallas kernels, attend_back(): pl.pallas_call(attend_back_kernel, grid=(width // PAIR,), in_specs=[colum...  16 us
  transfers between devices with their start and end apart: 34, of which 12 were waited for; matrix products, arithmetic and copies ran while one was open for 22% of the time, Pallas kernels for 7%

profile of v2, /device:TPU:0, one launch (start us, length us, event | category | flops | bytes accessed | tf_op | source)
XLA Modules:
  0.0 385.8 jit_solution(2353697402440768361)
XLA Ops:
  12.3 3.0 collective-permute-start
  15.3 2.6 collective-permute-start.1
  19.4 26.4 %all-gather.3.cloned.1.call-done = bf16[768,1152]{1,0:T(8,128)(2,1)} async-done(((bf16[192,1152]{1,0:T(8,128)(2,1)}), bf16[768,1152]{1,0:T(8,128)(2,1)}) %all-gather.3.cloned.1.call-update) | async-done | bytes 1769488 | tf_op jit(solution)/shard_map/all_gather | solution.py:204
  54.2 4.3 %broadcast_select_fusion.3 = (bf16[768,1152]{1,0:T(8,128)(2,1)}, bf16[768,1152]{1,0:T(8,128)(2,1)}) fusion(bf16[768,1152]{1,0:T(8,128)(2,1)} %all-gather.3.cloned.1.call-done, bf16[768,1152]{1,0:T(8,128)(2,1)} %collective-permute-done.3, pred[]{:T(512)S(6)} %eq.20), kind=kLoop, calls=%fused_computation.37 | loop fusion | flops 1769472 | bytes 7077889 | tf_op jit(solution)/shard_map/jit(_where)/select_n | solution.py:199
  58.5 3.9 fusion.4
  67.0 16.5 %all_gather.15 = bf16[768,384]{1,0:T(8,128)(2,1)S(1)} all-gather(bf16[192,384]{1,0:T(8,128)(2,1)S(1)} %constant_dynamic-slice_fusion.1), channel_id=1, replica_groups=mesh['seq'=4,'ctx'=8] {'seq'}, dimensions={0}, use_global_device_ids=true | all-gather | bytes 737280 | tf_op jit(solution)/shard_map/all_gather | solution.py:204
  85.8 2.4 collective-permute-start.12
  89.7 12.2 %all_gather.14 = bf16[1152,384]{1,0:T(8,128)(2,1)} all-gather(bf16[288,384]{1,0:T(8,128)(2,1)S(1)} %constant_dynamic-slice_fusion.2), channel_id=1, replica_groups=mesh['seq'=4,'ctx'=8] {'seq'}, dimensions={0}, use_global_device_ids=true | all-gather | bytes 1105920 | tf_op jit(solution)/shard_map/all_gather | solution.py:204
  107.6 10.1 %shard_map.143 = (bf16[384,768]{1,0:T(8,128)(2,1)S(1)}, f32[384,768]{1,0:T(8,128)S(1)}) custom-call(bf16[384,768]{1,0:T(8,128)(2,1)S(1)} %get-tuple-element.50.q_ref, bf16[768,768]{1,0:T(8,128)(2,1)S(1)} %pad_maximum_fusion.11.k_ref, bf16[768,768]{1,0:T(8,128)(2,1)} %pad_maximum_fusion.12.v_ref), custom_call_target="tpu_custom_call" | custom-call | flops 905969664 | bytes 7077888 | tf_op jit(solution)/shard_map/pallas_call | solution.py:69
  126.2 2.3 fusion.11
  130.3 2.4 convolution_convert_fusion.1
  134.9 2.4 fusion.98
  141.3 3.1 fusion
  144.4 4.3 %add_convert_fusion.1 = bf16[768,1152]{1,0:T(8,128)(2,1)} fusion(bf16[768,1152]{1,0:T(8,128)(2,1)} %collective-permute-done.15, bf16[384,768]{1,0:T(8,128)(2,1)S(1)} %fusion.41, s32[]{:T(128)S(6)} %select_n.217, bf16[384,1152]{1,0:T(8,128)(2,1)} %copy-done.59, bf16[384,1152]{1,0:T(8,128)(2,1)} %copy-done.60), kind=kOutput, calls=%fused_computation.3 | convolution fusion | flops 683900928 | bytes 5898244 | tf_op jit(solution)/shard_map/dot_general | solution.py:22
  149.1 3.2 fusion.17
  152.4 16.0 %shard_map.144 = (f32[384,768]{1,0:T(8,128)S(1)}, bf16[768,768]{1,0:T(8,128)(2,1)S(1)}, bf16[768,768]{1,0:T(8,128)(2,1)}) custom-call(bf16[384,768]{1,0:T(8,128)(2,1)S(1)} %copy-done.4, bf16[768,768]{1,0:T(8,128)(2,1)} %copy-done.2, bf16[768,768]{1,0:T(8,128)(2,1)} %pad_maximum_fusion.12.v_ref, bf16[384,768]{1,0:T(8,128)(2,1)S(1)} %convolution_convert_fusion.4.do_ref, ...), custom_call_target="tpu_custom_call" | custom-call | flops 2264924160 | bytes 10616832 | tf_op jit(solution)/shard_map/pallas_call | solution.py:90
  174.2 2.9 collective-permute-done.8
  177.8 9.0 %collective-permute-done.9 = bf16[96,768]{1,0:T(8,128)(2,1)S(1)} collective-permute-done((bf16[96,768]{1,0:T(8,128)(2,1)S(1)}, bf16[96,768]{1,0:T(8,128)(2,1)S(1)}, u32[]{:S(2)}, u32[]{:S(2)}) %collective-permute-start.9) | collective-permute-done | bytes 147488 | tf_op jit(solution)/shard_map/ppermute | solution.py:152
  194.1 2.6 fusion.34
  197.8 4.3 %convolution_convert_fusion = bf16[768,1152]{1,0:T(8,128)(2,1)} fusion(bf16[384,2304]{1,0:T(8,128)(2,1)S(1)} %pad_maximum_fusion.9, s32[]{:T(128)S(6)} %select_n.236, f32[384]{0:T(512)S(1)} %add_rsqrt_fusion.1, f32[384]{0:T(512)S(1)} %broadcast_multiply_fusion.6, bf16[96,768]{1,0:T(8,128)(2,1)} %collective-permute-done.2, ...), kind=kOutput, calls=%fused_computation.4 | convolution fusion | flops 683606016 | bytes 3248132 | tf_op jit(solution)/shard_map/dot_general | solution.py:22
  206.1 31.7 %reduce-scatter.9.cloned.1.call-done = bf16[192,1152]{1,0:T(8,128)(2,1)} async-done(((bf16[768,1152]{1,0:T(8,128)(2,1)}), bf16[192,1152]{1,0:T(8,128)(2,1)}) %reduce-scatter.9.cloned.1.call-update) | async-done | bytes 442384 | tf_op jit(solution)/shard_map/reduce_scatter | solution.py:216
  237.8 4.8 %fusion.96 = (f32[384]{0:T(512)S(1)}, f32[384]{0:T(512)S(1)}, f32[384,768]{1,0:T(8,128)}) fusion(f32[384]{0:T(512)S(1)} %add_rsqrt_fusion.1, f32[384]{0:T(512)S(1)} %broadcast_multiply_fusion.6, bf16[96,768]{1,0:T(8,128)(2,1)} %collective-permute-done.2, bf16[96,768]{1,0:T(8,128)(2,1)} %collective-permute-done.1, ...), kind=kOutput, calls=%fused_computation.207 | convolution fusion | flops 1375173888 | bytes 7084032 | tf_op jit(solution)/shard_map/dot_general | solution.py:22
  242.7 4.3 %add_convert_fusion = bf16[768,1152]{1,0:T(8,128)(2,1)} fusion(bf16[768,1152]{1,0:T(8,128)(2,1)} %collective-permute-done.21, bf16[384,2304]{1,0:T(8,128)(2,1)S(1)} %copy-done.27, s32[]{:T(128)S(6)} %select_n.217, f32[384]{0:T(512)S(1)} %add_rsqrt_fusion.1, f32[384]{0:T(512)S(1)} %broadcast_multiply_fusion.6, bf16[96,768]{1,0:T(8,128)(2,1)} %collective-permute-done.2, ...), kind=kOutput, calls=%fused_computation.2 | convolution fusion | flops 685375488 | bytes 5017604 | tf_op jit(solution)/shard_map/dot_general | solution.py:22
  249.8 3.4 collective-permute-start.18
  254.3 7.9 %collective-permute-done.18 = bf16[96,768]{1,0:T(8,128)(2,1)S(1)} collective-permute-done((bf16[96,768]{1,0:T(8,128)(2,1)S(1)}, bf16[96,768]{1,0:T(8,128)(2,1)S(1)}, u32[]{:S(2)}, u32[]{:S(2)}) %collective-permute-start.18) | collective-permute-done | bytes 147488 | tf_op jit(solution)/shard_map/ppermute | solution.py:152
  262.1 12.6 %collective-permute-done.19 = bf16[96,768]{1,0:T(8,128)(2,1)S(1)} collective-permute-done((bf16[96,768]{1,0:T(8,128)(2,1)S(1)}, bf16[96,768]{1,0:T(8,128)(2,1)S(1)}, u32[]{:S(2)}, u32[]{:S(2)}) %collective-permute-start.19) | collective-permute-done | bytes 147488 | tf_op jit(solution)/shard_map/ppermute | solution.py:152
  274.8 21.1 %all-reduce.6.cloned.1.call-done = (bf16[288,384]{1,0:T(8,128)(2,1)}, bf16[192,1152]{1,0:T(8,128)(2,1)}, bf16[192,384]{1,0:T(8,128)(2,1)}) async-done(((bf16[288,384]{1,0:T(8,128)(2,1)}, bf16[192,1152]{1,0:T(8,128)(2,1)}, bf16[192,384]{1,0:T(8,128)(2,1)}), (bf16[288,384]{1,0:T(8,128)(2,1)}, bf16[192,1152]{1,0:T(8,128)(2,1)}, bf16[192,384]{1,0:T(8,128)(2,1)})) %all-reduce.6.cloned.1.call-update) | async-done | bytes 811024 | tf_op jit(solution)/shard_map/psum | solution.py:219
  300.5 30.9 %reduce-scatter.5.cloned.1.call-done = bf16[192,1152]{1,0:T(8,128)(2,1)} async-done(((bf16[768,1152]{1,0:T(8,128)(2,1)}), bf16[192,1152]{1,0:T(8,128)(2,1)}) %reduce-scatter.5.cloned.1.call-update) | async-done | bytes 442384 | tf_op jit(solution)/shard_map/reduce_scatter | solution.py:216
  332.8 38.5 %all-reduce.4.cloned.1.call-done = bf16[192,1152]{1,0:T(8,128)(2,1)} async-done(((bf16[192,1152]{1,0:T(8,128)(2,1)}), bf16[192,1152]{1,0:T(8,128)(2,1)}) %all-reduce.4.cloned.1.call-update) | async-done | bytes 442384 | tf_op jit(solution)/shard_map/psum | solution.py:219
  371.3 2.2 dynamic-slice_convert_fusion
  373.5 2.1 multiply_reduce_fusion
  376.8 2.2 fusion.5
  (274 shorter events, 75.4 us)
Async XLA Ops:
  7.2 38.6 %all-gather.3.cloned.1.call-start = ((), (), s32[]{:S(2)}) async-start(), calls=%async_computation.4 | async-start | bytes 2211840 | tf_op jit(solution)/shard_map/all_gather | solution.py:204
  10.2 108.6 %all-gather.5.cloned.1.call-start = ((), (), s32[]{:S(2)}) async-start(), calls=%async_computation.5 | async-start | bytes 2211840 | tf_op jit(solution)/shard_map/all_gather | solution.py:204
  12.3 38.9 %collective-permute-start = (bf16[96,768]{1,0:T(8,128)(2,1)}, bf16[96,768]{1,0:T(8,128)(2,1)}, u32[]{:S(2)}, u32[]{:S(2)}) collective-permute-start(bf16[96,768]{1,0:T(8,128)(2,1)} %get-tuple-element.104), channel_id=1, source_target_pairs={{0,2},{1,3},{2,4},{3,5},{4,6},{5,7},{6,0},{7,1},{8,10},{9,11},{10,... | collective-permute-start | bytes 442376 | tf_op jit(solution)/shard_map/ppermute | solution.py:152
  15.3 35.9 %collective-permute-start.1 = (bf16[96,768]{1,0:T(8,128)(2,1)}, bf16[96,768]{1,0:T(8,128)(2,1)}, u32[]{:S(2)}, u32[]{:S(2)}) collective-permute-start(bf16[96,768]{1,0:T(8,128)(2,1)} %get-tuple-element.106), channel_id=1, source_target_pairs={{0,4},{1,5},{2,6},{3,7},{4,0},{5,1},{6,2},{7,3},{8,12},{9,13},{10,... | collective-permute-start | bytes 442376 | tf_op jit(solution)/shard_map/ppermute | solution.py:152
  17.9 33.3 %collective-permute-start.2 = (bf16[96,768]{1,0:T(8,128)(2,1)}, bf16[96,768]{1,0:T(8,128)(2,1)}, u32[]{:S(2)}, u32[]{:S(2)}) collective-permute-start(bf16[96,768]{1,0:T(8,128)(2,1)} %get-tuple-element.105), channel_id=1, source_target_pairs={{0,6},{1,7},{2,0},{3,1},{4,2},{5,3},{6,4},{7,5},{8,14},{9,15},{10,... | collective-permute-start | bytes 442376 | tf_op jit(solution)/shard_map/ppermute | solution.py:152
  45.8 8.4 %collective-permute-start.3 = (bf16[768,1152]{1,0:T(8,128)(2,1)}, bf16[768,1152]{1,0:T(8,128)(2,1)}, u32[]{:S(2)}, u32[]{:S(2)}) collective-permute-start(bf16[768,1152]{1,0:T(8,128)(2,1)} %all-gather.3.cloned.1.call-done), channel_id=1, source_target_pairs={{0,1},{1,0},{2,3},{3,2},{4,5},{5,4},{6,7},{7,6},{8,9},{9,8},{10,11... | collective-permute-start | bytes 5308424 | tf_op jit(solution)/shard_map/ppermute | solution.py:207
  46.7 159.4 %reduce-scatter.11.cloned.1.call-start = ((), (), s32[]{:S(2)}) async-start(), calls=%async_computation.9 | async-start | bytes 737280 | tf_op jit(solution)/shard_map/reduce_scatter | solution.py:216
  66.5 38.6 %collective-permute-start.4 = (bf16[2,384,768]{2,1,0:T(8,128)(2,1)}, bf16[2,384,768]{2,1,0:T(8,128)(2,1)S(1)}, u32[]{:S(2)}, u32[]{:S(2)}) collective-permute-start(bf16[2,384,768]{2,1,0:T(8,128)(2,1)} %pad_maximum_fusion.10), channel_id=1, source_target_pairs={{0,1},{1,0},{2,3},{3,2},{4,5},{5,4},{6,7},{7,6},{8,9},{9,8},{10,11... | collective-permute-start | bytes 3538952 | tf_op jit(solution)/shard_map/ppermute | solution.py:173
  83.5 35.2 %collective-permute-start.5 = (bf16[768,384]{1,0:T(8,128)(2,1)S(1)}, bf16[768,384]{1,0:T(8,128)(2,1)}, u32[]{:S(2)}, u32[]{:S(2)}) collective-permute-start(bf16[768,384]{1,0:T(8,128)(2,1)S(1)} %all_gather.15), channel_id=1, source_target_pairs={{0,1},{1,0},{2,3},{3,2},{4,5},{5,4},{6,7},{7,6},{8,9},{9,8},{10,11... | collective-permute-start | bytes 1769480 | tf_op jit(solution)/shard_map/ppermute | solution.py:207
  84.3 17.5 %collective-permute-start.11 = (bf16[96,768]{1,0:T(8,128)(2,1)}, bf16[96,768]{1,0:T(8,128)(2,1)S(1)}, u32[]{:S(2)}, u32[]{:S(2)}) collective-permute-start(bf16[96,768]{1,0:T(8,128)(2,1)} %get-tuple-element.97), channel_id=1, source_target_pairs={{0,2},{1,3},{2,4},{3,5},{4,6},{5,7},{6,0},{7,1},{8,10},{9,11},{10,... | collective-permute-start | bytes 442376 | tf_op jit(solution)/shard_map/ppermute | solution.py:152
  85.8 16.1 %collective-permute-start.12 = (bf16[96,768]{1,0:T(8,128)(2,1)}, bf16[96,768]{1,0:T(8,128)(2,1)S(1)}, u32[]{:S(2)}, u32[]{:S(2)}) collective-permute-start(bf16[96,768]{1,0:T(8,128)(2,1)} %get-tuple-element.99), channel_id=1, source_target_pairs={{0,4},{1,5},{2,6},{3,7},{4,0},{5,1},{6,2},{7,3},{8,12},{9,13},{10,... | collective-permute-start | bytes 442376 | tf_op jit(solution)/shard_map/ppermute | solution.py:152
  88.2 13.7 %collective-permute-start.13 = (bf16[96,768]{1,0:T(8,128)(2,1)}, bf16[96,768]{1,0:T(8,128)(2,1)}, u32[]{:S(2)}, u32[]{:S(2)}) collective-permute-start(bf16[96,768]{1,0:T(8,128)(2,1)} %get-tuple-element.98), channel_id=1, source_target_pairs={{0,6},{1,7},{2,0},{3,1},{4,2},{5,3},{6,4},{7,5},{8,14},{9,15},{10,... | collective-permute-start | bytes 442376 | tf_op jit(solution)/shard_map/ppermute | solution.py:152
  118.8 5.2 %collective-permute-start.6 = (bf16[768,1152]{1,0:T(8,128)(2,1)}, bf16[768,1152]{1,0:T(8,128)(2,1)S(1)}, u32[]{:S(2)}, u32[]{:S(2)}) collective-permute-start(bf16[768,1152]{1,0:T(8,128)(2,1)} %all-gather.5.cloned.1.call-done), channel_id=1, source_target_pairs={{0,1},{1,0},{2,3},{3,2},{4,5},{5,4},{6,7},{7,6},{8,9},{9,8},{10,11... | collective-permute-start | bytes 5308424 | tf_op jit(solution)/shard_map/ppermute | solution.py:207
  120.1 3.6 collective-permute-start.7
  132.7 11.7 %collective-permute-start.15 = (bf16[768,1152]{1,0:T(8,128)(2,1)}, bf16[768,1152]{1,0:T(8,128)(2,1)}, u32[]{:S(2)}, u32[]{:S(2)}) collective-permute-start(bf16[768,1152]{1,0:T(8,128)(2,1)} %convolution_convert_fusion.1), channel_id=1, source_target_pairs={{0,1},{1,0},{2,3},{3,2},{4,5},{5,4},{6,7},{7,6},{8,9},{9,8},{10,11... | collective-permute-start | bytes 5308424 | tf_op jit(solution)/shard_map/ppermute | solution.py:211
  134.5 6.8 %collective-permute-start.14 = (bf16[1152,384]{1,0:T(8,128)(2,1)}, bf16[1152,384]{1,0:T(8,128)(2,1)}, u32[]{:S(2)}, u32[]{:S(2)}) collective-permute-start(bf16[1152,384]{1,0:T(8,128)(2,1)} %convolution_convert_fusion.2), channel_id=1, source_target_pairs={{0,1},{1,0},{2,3},{3,2},{4,5},{5,4},{6,7},{7,6},{8,9},{9,8},{10,11... | collective-permute-start | bytes 2654216 | tf_op jit(solution)/shard_map/ppermute | solution.py:211
  148.8 57.3 %reduce-scatter.7.cloned.1.call-start = ((), (), s32[]{:S(2)}) async-start(), calls=%async_computation.7 | async-start | bytes 1105920 | tf_op jit(solution)/shard_map/reduce_scatter | solution.py:216
  152.3 85.4 %reduce-scatter.9.cloned.1.call-start = ((), (), s32[]{:S(2)}) async-start(), calls=%async_computation.8 | async-start | bytes 2211840 | tf_op jit(solution)/shard_map/reduce_scatter | solution.py:216
  170.7 19.8 %collective-permute-start.17 = (bf16[2,384,768]{2,1,0:T(8,128)(2,1)}, bf16[2,384,768]{2,1,0:T(8,128)(2,1)}, u32[]{:S(2)}, u32[]{:S(2)}) collective-permute-start(bf16[2,384,768]{2,1,0:T(8,128)(2,1)} %pad_maximum_fusion.14), channel_id=1, source_target_pairs={{0,1},{1,0},{2,3},{3,2},{4,5},{5,4},{6,7},{7,6},{8,9},{9,8},{10,11... | collective-permute-start | bytes 3538952 | tf_op jit(solution)/shard_map/ppermute | solution.py:181
  170.9 6.2 %collective-permute-start.8 = (bf16[96,768]{1,0:T(8,128)(2,1)S(1)}, bf16[96,768]{1,0:T(8,128)(2,1)S(1)}, u32[]{:S(2)}, u32[]{:S(2)}) collective-permute-start(bf16[96,768]{1,0:T(8,128)(2,1)S(1)} %get-tuple-element.102), channel_id=1, source_target_pairs={{0,6},{1,7},{2,0},{3,1},{4,2},{5,3},{6,4},{7,5},{8,14},{9,15},{10,... | collective-permute-start | bytes 442376 | tf_op jit(solution)/shard_map/ppermute | solution.py:152
  172.6 14.2 %collective-permute-start.9 = (bf16[96,768]{1,0:T(8,128)(2,1)S(1)}, bf16[96,768]{1,0:T(8,128)(2,1)S(1)}, u32[]{:S(2)}, u32[]{:S(2)}) collective-permute-start(bf16[96,768]{1,0:T(8,128)(2,1)S(1)} %get-tuple-element.101), channel_id=1, source_target_pairs={{0,4},{1,5},{2,6},{3,7},{4,0},{5,1},{6,2},{7,3},{8,12},{9,13},{10,... | collective-permute-start | bytes 442376 | tf_op jit(solution)/shard_map/ppermute | solution.py:152
  173.2 14.3 %collective-permute-start.10 = (bf16[96,768]{1,0:T(8,128)(2,1)S(1)}, bf16[96,768]{1,0:T(8,128)(2,1)S(1)}, u32[]{:S(2)}, u32[]{:S(2)}) collective-permute-start(bf16[96,768]{1,0:T(8,128)(2,1)S(1)} %get-tuple-element.100), channel_id=1, source_target_pairs={{0,2},{1,3},{2,4},{3,5},{4,6},{5,7},{6,0},{7,1},{8,10},{9,11},{10,... | collective-permute-start | bytes 442376 | tf_op jit(solution)/shard_map/ppermute | solution.py:152
  188.9 107.0 %all-reduce.6.cloned.1.call-start = ((), (), s32[]{:S(2)}) async-start(), calls=%async_computation.11 | async-start | bytes 1622016 | tf_op jit(solution)/shard_map/psum | solution.py:219
  202.1 40.5 %collective-permute-start.21 = (bf16[768,1152]{1,0:T(8,128)(2,1)}, bf16[768,1152]{1,0:T(8,128)(2,1)}, u32[]{:S(2)}, u32[]{:S(2)}) collective-permute-start(bf16[768,1152]{1,0:T(8,128)(2,1)} %convolution_convert_fusion), channel_id=1, source_target_pairs={{0,1},{1,0},{2,3},{3,2},{4,5},{5,4},{6,7},{7,6},{8,9},{9,8},{10,11... | collective-permute-start | bytes 5308424 | tf_op jit(solution)/shard_map/ppermute | solution.py:211
  237.8 93.7 %reduce-scatter.5.cloned.1.call-start = ((), (), s32[]{:S(2)}) async-start(), calls=%async_computation.6 | async-start | bytes 2211840 | tf_op jit(solution)/shard_map/reduce_scatter | solution.py:216
  247.0 124.3 %all-reduce.4.cloned.1.call-start = ((), (), s32[]{:S(2)}) async-start(), calls=%async_computation.10 | async-start | bytes 884736 | tf_op jit(solution)/shard_map/psum | solution.py:219
  249.8 12.4 %collective-permute-start.18 = (bf16[96,768]{1,0:T(8,128)(2,1)S(1)}, bf16[96,768]{1,0:T(8,128)(2,1)S(1)}, u32[]{:S(2)}, u32[]{:S(2)}) collective-permute-start(bf16[96,768]{1,0:T(8,128)(2,1)S(1)} %get-tuple-element.95), channel_id=1, source_target_pairs={{0,6},{1,7},{2,0},{3,1},{4,2},{5,3},{6,4},{7,5},{8,14},{9,15},{10,... | collective-permute-start | bytes 442376 | tf_op jit(solution)/shard_map/ppermute | solution.py:152
  253.1 21.6 %collective-permute-start.19 = (bf16[96,768]{1,0:T(8,128)(2,1)S(1)}, bf16[96,768]{1,0:T(8,128)(2,1)S(1)}, u32[]{:S(2)}, u32[]{:S(2)}) collective-permute-start(bf16[96,768]{1,0:T(8,128)(2,1)S(1)} %get-tuple-element.94), channel_id=1, source_target_pairs={{0,4},{1,5},{2,6},{3,7},{4,0},{5,1},{6,2},{7,3},{8,12},{9,13},{10,... | collective-permute-start | bytes 442376 | tf_op jit(solution)/shard_map/ppermute | solution.py:152
  253.1 21.6 %collective-permute-start.20 = (bf16[96,768]{1,0:T(8,128)(2,1)S(1)}, bf16[96,768]{1,0:T(8,128)(2,1)S(1)}, u32[]{:S(2)}, u32[]{:S(2)}) collective-permute-start(bf16[96,768]{1,0:T(8,128)(2,1)S(1)} %get-tuple-element.93), channel_id=1, source_target_pairs={{0,2},{1,3},{2,4},{3,5},{4,6},{5,7},{6,0},{7,1},{8,10},{9,11},{10,... | collective-permute-start | bytes 442376 | tf_op jit(solution)/shard_map/ppermute | solution.py:152
  296.0 4.3 %collective-permute-start.23 = (bf16[192,1152]{1,0:T(8,128)(2,1)}, bf16[192,1152]{1,0:T(8,128)(2,1)S(1)}, u32[]{:S(2)}, u32[]{:S(2)}) collective-permute-start(bf16[192,1152]{1,0:T(8,128)(2,1)} %get-tuple-element.45), channel_id=1, source_target_pairs={{0,1},{1,0},{2,3},{3,2},{4,5},{5,4},{6,7},{7,6},{8,9},{9,8},{10,11... | collective-permute-start | bytes 1327112 | tf_op jit(solution)/shard_map/ppermute | solution.py:220
  296.5 2.8 collective-permute-start.22
  371.3 4.3 %collective-permute-start.25 = (bf16[192,1152]{1,0:T(8,128)(2,1)}, bf16[192,1152]{1,0:T(8,128)(2,1)S(1)}, u32[]{:S(2)}, u32[]{:S(2)}) collective-permute-start(bf16[192,1152]{1,0:T(8,128)(2,1)} %all-reduce.4.cloned.1.call-done), channel_id=1, source_target_pairs={{0,1},{1,0},{2,3},{3,2},{4,5},{5,4},{6,7},{7,6},{8,9},{9,8},{10,11... | collective-permute-start | bytes 1327112 | tf_op jit(solution)/shard_map/ppermute | solution.py:220
  (63 other events, 512.5 us)
Sparse Core Ops, SparseCore 0:
  10.4 35.2 all-gather.2
  48.2 37.2 all-gather.4
  148.9 23.4 reduce-scatter.10
  175.4 26.6 reduce-scatter.6
  205.2 32.4 reduce-scatter.8
  240.4 55.4 all-reduce.5
  299.8 31.6 reduce-scatter.4
  333.9 37.3 all-reduce.3

commit v3 on v2

--- a/solution.py
+++ b/solution.py
@@ -215,16 +215,35 @@
     def scatter(kept):
         return lax.psum_scatter(kept, "seq", scatter_dimension=0, tiled=True)
 
-    def reduce_ctx(parts):
-        totals = lax.psum(parts, "ctx", axis_index_groups=parity)
-        return [join(t, lax.ppermute(t, "ctx", swap)).astype(f32) for t in totals]
+    mlp_rows, attn_rows = w_mlp.shape[0], w_attn.shape[0]
+    narrow = width // 2
+
+    def pack(mlp, attn, wide):
+        wide = wide.reshape(-1, attn_rows, wide.shape[1])
+        blocks = [wide[:, :, i : i + narrow] for i in range(0, wide.shape[2], narrow)]
+        rows = [mlp.reshape(-1, mlp_rows, narrow), attn.reshape(-1, attn_rows, narrow)]
+        return jnp.concatenate(rows + blocks, axis=1)
+
+    def unpack(packed):
+        start = mlp_rows + attn_rows
+        ends = range(start, packed.shape[1], attn_rows)
+        blocks = [packed[:, i : i + attn_rows].reshape(-1, narrow) for i in ends]
+        return (
+            packed[:, :mlp_rows].reshape(-1, narrow),
+            packed[:, mlp_rows:start].reshape(-1, narrow),
+            jnp.concatenate(blocks, axis=1),
+        )
+
+    def join_packed(own):
+        other = lax.ppermute(own, "ctx", swap)
+        return [join(a, b) for a, b in zip(unpack(own), unpack(other))]
 
     gain_one = gain_one.astype(f32)[:, None]
     gain_two = gain_two.astype(f32)[:, None]
     qkv_all = both_halves(gather((w_qkv.astype(f32) * gain_one).astype(bf16)))
-    attn_all = gather(w_attn)
-    in_all = gather((w_in.astype(f32) * gain_two).astype(bf16))
-    mlp_all = gather(w_mlp)
+    scaled_in = (w_in.astype(f32) * gain_two).astype(bf16)
+    packed = pack(half_of(w_mlp, core), half_of(w_attn, core), half_of(scaled_in, core))
+    packed = lax.all_gather(packed, "seq", axis=0, tiled=True)
 
     x = to_sequence(tokens).astype(f32)
     g = to_sequence(cotangent)
@@ -244,10 +263,9 @@
     k = rotate(qkv[:, width : 2 * width], cosines, sines).astype(bf16)
     v = qkv[:, 2 * width :].astype(bf16)
     keys, values = share_keys(k, v)
-    attn_all = both_halves(attn_all)
     attn, lse = attend(q, keys, values)
-    attn, in_all, mlp_all = lax.optimization_barrier((attn, in_all, mlp_all))
-    in_all, mlp_all = both_halves(in_all), both_halves(mlp_all)
+    attn, packed = lax.optimization_barrier((attn, packed))
+    mlp_all, attn_all, in_all = join_packed(packed)
     x2 = x + dot(attn, attn_all, NN)
     xhat2, scale_two = normalize(x2)
     h2 = xhat2.astype(bf16)
@@ -266,19 +284,18 @@
     dy = dx2.astype(bf16)
     part_attn = reduce_pair(attn, dy)
     do = dot(dy, attn_all, NT).astype(bf16)
-    do, part_mlp, part_in, part_attn = lax.optimization_barrier((do, part_mlp, part_in, part_attn))
-    parts = [scatter(part_mlp), scatter(part_in), scatter(part_attn)]
-    grad_mlp, raw_in, grad_attn = reduce_ctx(parts)
+    part = pack(part_mlp, part_attn, part_in)
+    do, part = lax.optimization_barrier((do, part))
+    part = lax.psum(scatter(part), "ctx", axis_index_groups=parity)
     dq, dk, dv = attend_back(q, keys, values, do, lse)
     dk, dv = sum_keys(dk, dv)
     dqkv = jnp.concatenate(
         [unrotate(dq, cosines, sines), unrotate(dk, cosines, sines), dv], axis=-1
     ).astype(bf16)
     part_qkv = scatter(reduce_pair(h1, dqkv))
-    part_qkv, grad_mlp, raw_in, grad_attn = lax.optimization_barrier(
-        (part_qkv, grad_mlp, raw_in, grad_attn)
-    )
-    (raw_qkv,) = reduce_ctx([part_qkv])
+    part_qkv, part = lax.optimization_barrier((part_qkv, part))
+    raw_qkv = both_halves(lax.psum(part_qkv, "ctx", axis_index_groups=parity)).astype(f32)
+    grad_mlp, grad_attn, raw_in = [t.astype(f32) for t in join_packed(part)]
     dx = dx2 + norm_back(dot(dqkv, qkv_all, NT), xhat, scale_one)
     grad_tokens = from_sequence(dx.astype(bf16)).astype(f32)
     return (

time: 387 us -> 318 us (0.82)
  blocking collectives: 28.7 us -> 0 us
  waiting for transfers between devices: 184 us -> 172 us
  matrix products: 42 us -> 30.3 us
  local copies, waits for them, and re-layouts: 29.3 us -> 20.7 us
  other arithmetic: 38.3 us -> 31 us
    reduce_scatter x4 -> x1, waiting for transfers between devices: 62.6 us -> 4.94 us  [scatter(): return lax.psum_scatter(kept, 'seq', scatter_dimension=0, tiled=True)]
    all_gather x2 -> x0, blocking collectives: 28.7 us -> none  [gather(): return lax.all_gather(half_of(shard, core), 'seq', axis=0, tiled=True)]
    psum x2, waiting for transfers between devices: 59.6 us -> 84.4 us  [the longest x1 46.8 us: body(): part = lax.psum(scatter(part), 'ctx', axis_index_groups=parity)]
    all_gather x0 -> x1, waiting for transfers between devices: none -> 15.8 us  [body(): packed = lax.all_gather(packed, 'seq', axis=0, tiled=True)]
    dot_general x16, matrix products: 42 us -> 30.3 us  [dot(): return lax.dot_general(a, b, (dims, ((), ())), preferred_element_type=f32)]
    unnamed x136 -> x112, local copies, waits for them, and re-layouts: 15.2 us -> 11.7 us
    all_gather x2 -> x1, waiting for transfers between devices: 26.4 us -> 25.5 us  [gather(): return lax.all_gather(half_of(shard, core), 'seq', axis=0, tiled=True)]
  transfers between devices with their start and end apart: 34 -> 28, of which waited for: 12 -> 15; matrix products, arithmetic and copies ran while one was open for 22% -> 16% of each run, Pallas kernels for 7% -> 8%
where the time goes in v3:
time: 318 us; the launch traced here: 317 us
  waiting for transfers between devices  172 us (54%)
  other arithmetic  31 us (10%)
  matrix products  30.3 us (10%)
  Pallas kernels  25.8 us (8%)
  starting transfers between devices  22.1 us (7%)
  local copies, waits for them, and re-layouts  20.7 us (7%)
  between operations  15.2 us (5%)
    psum x1, waiting for transfers between devices, body(): part = lax.psum(scatter(part), 'ctx', axis_index_groups=parity)  46.8 us
    psum x1, waiting for transfers between devices, body(): lax.psum(part_qkv, 'ctx', axis_index_groups=parity)  37.6 us
    ppermute x12, waiting for transfers between devices, hop(): return lax.ppermute(block, 'ctx', route)  33.1 us
    dot_general x16, matrix products, dot(): return lax.dot_general(a, b, (dims, ((), ())), preferred_element_type=f32)  30.3 us
    all_gather x1, waiting for transfers between devices, gather(): return lax.all_gather(half_of(shard, core), 'seq', axis=0, tiled=True)  25.5 us
    ppermute x12, starting transfers between devices, hop(): return lax.ppermute(block, 'ctx', route)  19.9 us
    pallas_call x1, Pallas kernels, attend_back(): pl.pallas_call(attend_back_kernel, grid=(width // PAIR,), in_specs=[colum...  15.9 us
    all_gather x1, waiting for transfers between devices, body(): packed = lax.all_gather(packed, 'seq', axis=0, tiled=True)  15.8 us
  transfers between devices with their start and end apart: 28, of which 15 were waited for; matrix products, arithmetic and copies ran while one was open for 16% of the time, Pallas kernels for 8%

profile of v3, /device:TPU:0, one launch (start us, length us, event | category | flops | bytes accessed | tf_op | source)
XLA Modules:
  0.0 317.0 jit_solution(4978151949501545065)
XLA Ops:
  11.1 3.0 collective-permute-start
  14.1 2.6 collective-permute-start.1
  20.3 25.5 %all-gather.3.cloned.1.call-done = bf16[768,1152]{1,0:T(8,128)(2,1)} async-done(((bf16[192,1152]{1,0:T(8,128)(2,1)}), bf16[768,1152]{1,0:T(8,128)(2,1)}) %all-gather.3.cloned.1.call-update) | async-done | bytes 1769488 | tf_op jit(solution)/shard_map/all_gather | solution.py:204
  53.4 2.6 broadcast_select_fusion.3
  56.0 3.2 %fusion.4 = f32[384,2304]{1,0:T(8,128)S(1)} fusion(bf16[768,1152]{1,0:T(8,128)(2,1)S(1)} %get-tuple-element.56, bf16[768,1152]{1,0:T(8,128)(2,1)S(1)} %get-tuple-element.55, f32[384]{0:T(512)S(1)} %add_rsqrt_fusion.1, f32[384]{0:T(512)S(1)} %broadcast_multiply_fusion.5, bf16[96,768]{1,0:T(8,128)(2,1)} %collective-permute-done.2, ...), kind=kOutput, calls=%fused_computation.13 | convolution fusion | flops 1369276416 | bytes 7670784 | tf_op jit(solution)/shard_map/dot_general | solution.py:22
  62.3 2.4 collective-permute-done.4
  66.2 9.9 %shard_map.143 = (bf16[384,768]{1,0:T(8,128)(2,1)S(1)}, f32[384,768]{1,0:T(8,128)S(1)}) custom-call(bf16[384,768]{1,0:T(8,128)(2,1)S(1)} %get-tuple-element.41.q_ref, bf16[768,768]{1,0:T(8,128)(2,1)S(1)} %pad_maximum_fusion.13.k_ref, bf16[768,768]{1,0:T(8,128)(2,1)} %pad_maximum_fusion.14.v_ref), custom_call_target="tpu_custom_call" | custom-call | flops 905969664 | bytes 7077888 | tf_op jit(solution)/shard_map/pallas_call | solution.py:69
  77.2 15.8 %all-gather.5.cloned.1.call-done = bf16[4,1056,384]{2,1,0:T(8,128)(2,1)} async-done(((bf16[1,1056,384]{2,1,0:T(8,128)(2,1)}), bf16[4,1056,384]{2,1,0:T(8,128)(2,1)}) %all-gather.5.cloned.1.call-update) | async-done | bytes 3244048 | tf_op jit(solution)/shard_map/all_gather | solution.py:246
  94.2 2.5 collective-permute-start.10
  98.7 6.3 %collective-permute-done.10 = bf16[96,768]{1,0:T(8,128)(2,1)S(1)} collective-permute-done((bf16[96,768]{1,0:T(8,128)(2,1)S(1)}, bf16[96,768]{1,0:T(8,128)(2,1)S(1)}, u32[]{:S(2)}, u32[]{:S(2)}) %collective-permute-start.10) | collective-permute-done | bytes 147488 | tf_op jit(solution)/shard_map/ppermute | solution.py:152
  105.0 3.8 %collective-permute-done.9 = bf16[96,768]{1,0:T(8,128)(2,1)S(1)} collective-permute-done((bf16[96,768]{1,0:T(8,128)(2,1)S(1)}, bf16[96,768]{1,0:T(8,128)(2,1)S(1)}, u32[]{:S(2)}, u32[]{:S(2)}) %collective-permute-start.9) | collective-permute-done | bytes 147488 | tf_op jit(solution)/shard_map/ppermute | solution.py:152
  108.8 2.9 fusion.103
  111.7 1.8 fusion.111
  119.4 1.7 fusion.99
  135.7 15.9 %shard_map.144 = (f32[384,768]{1,0:T(8,128)S(1)}, bf16[768,768]{1,0:T(8,128)(2,1)S(1)}, bf16[768,768]{1,0:T(8,128)(2,1)}) custom-call(bf16[384,768]{1,0:T(8,128)(2,1)S(1)} %get-tuple-element.41.q_ref, bf16[768,768]{1,0:T(8,128)(2,1)} %copy-done, bf16[768,768]{1,0:T(8,128)(2,1)} %pad_maximum_fusion.14.v_ref, ...), custom_call_target="tpu_custom_call" | custom-call | flops 2264924160 | bytes 10616832 | tf_op jit(solution)/shard_map/pallas_call | solution.py:90
  153.1 2.7 collective-permute-done.15
  160.3 4.3 %convolution_convert_fusion = bf16[768,1152]{1,0:T(8,128)(2,1)} fusion(bf16[384,2304]{1,0:T(8,128)(2,1)S(1)} %pad_maximum_fusion.11, s32[]{:T(128)S(6)} %select_n.264, f32[384]{0:T(512)S(1)} %add_rsqrt_fusion.1, f32[384]{0:T(512)S(1)} %broadcast_multiply_fusion.5, bf16[96,768]{1,0:T(8,128)(2,1)} %collective-permute-done.2, ...), kind=kOutput, calls=%fused_computation.4 | convolution fusion | flops 683606016 | bytes 3248132 | tf_op jit(solution)/shard_map/dot_general | solution.py:22
  164.7 2.5 fusion.18
  168.6 4.8 %add_convert_fusion = bf16[768,1152]{1,0:T(8,128)(2,1)} fusion(bf16[768,1152]{1,0:T(8,128)(2,1)} %collective-permute-done.19, bf16[384,2304]{1,0:T(8,128)(2,1)S(1)} %copy-done.21, s32[]{:T(128)S(6)} %select_n.241, f32[384]{0:T(512)S(1)} %add_rsqrt_fusion.1, f32[384]{0:T(512)S(1)} %broadcast_multiply_fusion.5, bf16[96,768]{1,0:T(8,128)(2,1)} %collective-permute-done.2, ...), kind=kOutput, calls=%fused_computation.2 | convolution fusion | flops 685375488 | bytes 5017604 | tf_op jit(solution)/shard_map/dot_general | solution.py:22
  173.5 2.1 collective-permute-start.6
  175.6 2.0 collective-permute-start.7
  177.7 1.9 collective-permute-start.8
  180.0 11.2 %collective-permute-done.7 = bf16[96,768]{1,0:T(8,128)(2,1)S(1)} collective-permute-done((bf16[96,768]{1,0:T(8,128)(2,1)S(1)}, bf16[96,768]{1,0:T(8,128)(2,1)S(1)}, u32[]{:S(2)}, u32[]{:S(2)}) %collective-permute-start.7) | collective-permute-done | bytes 147488 | tf_op jit(solution)/shard_map/ppermute | solution.py:152
  193.2 3.4 %fusion.98 = (f32[384]{0:T(512)S(1)}, f32[384]{0:T(512)S(1)}, f32[384,768]{1,0:T(8,128)S(1)}) fusion(f32[384]{0:T(512)S(1)} %add_rsqrt_fusion.1, f32[384]{0:T(512)S(1)} %broadcast_multiply_fusion.5, bf16[96,768]{1,0:T(8,128)(2,1)} %collective-permute-done.2, bf16[96,768]{1,0:T(8,128)(2,1)} %collective-permute-done.1, ...), kind=kOutput, calls=%fused_computation.227 | convolution fusion | flops 1375173888 | bytes 7084032 | tf_op jit(solution)/shard_map/dot_general | solution.py:22
  198.5 1.9 collective-permute-start.18
  200.6 4.4 %collective-permute-done.16 = bf16[96,768]{1,0:T(8,128)(2,1)S(1)} collective-permute-done((bf16[96,768]{1,0:T(8,128)(2,1)S(1)}, bf16[96,768]{1,0:T(8,128)(2,1)S(1)}, u32[]{:S(2)}, u32[]{:S(2)}) %collective-permute-start.16) | collective-permute-done | bytes 147488 | tf_op jit(solution)/shard_map/ppermute | solution.py:152
  205.0 7.0 %collective-permute-done.17 = bf16[96,768]{1,0:T(8,128)(2,1)S(1)} collective-permute-done((bf16[96,768]{1,0:T(8,128)(2,1)S(1)}, bf16[96,768]{1,0:T(8,128)(2,1)S(1)}, u32[]{:S(2)}, u32[]{:S(2)}) %collective-permute-start.17) | collective-permute-done | bytes 147488 | tf_op jit(solution)/shard_map/ppermute | solution.py:152
  212.0 4.9 %reduce-scatter.5.cloned.1.call-done = bf16[192,1152]{1,0:T(8,128)(2,1)} async-done(((bf16[768,1152]{1,0:T(8,128)(2,1)}), bf16[192,1152]{1,0:T(8,128)(2,1)}) %reduce-scatter.5.cloned.1.call-update) | async-done | bytes 442384 | tf_op jit(solution)/shard_map/reduce_scatter | solution.py:216
  217.0 46.8 %all-reduce.4.cloned.1.call-done = bf16[1,1056,384]{2,1,0:T(8,128)(2,1)} async-done(((bf16[1,1056,384]{2,1,0:T(8,128)(2,1)}), bf16[1,1056,384]{2,1,0:T(8,128)(2,1)}) %all-reduce.4.cloned.1.call-update) | async-done | bytes 811024 | tf_op jit(solution)/shard_map/psum | solution.py:289
  265.0 37.6 %all-reduce.6.cloned.1.call-done = bf16[192,1152]{1,0:T(8,128)(2,1)} async-done(((bf16[192,1152]{1,0:T(8,128)(2,1)}), bf16[192,1152]{1,0:T(8,128)(2,1)}) %all-reduce.6.cloned.1.call-update) | async-done | bytes 442384 | tf_op jit(solution)/shard_map/psum | solution.py:297
  305.8 2.2 fusion.6
  308.0 2.2 fusion.5
  (232 shorter events, 59.9 us)
Async XLA Ops:
  7.2 38.6 %all-gather.3.cloned.1.call-start = ((), (), s32[]{:S(2)}) async-start(), calls=%async_computation.2 | async-start | bytes 2211840 | tf_op jit(solution)/shard_map/all_gather | solution.py:204
  10.1 82.9 %all-gather.5.cloned.1.call-start = ((), (), s32[]{:S(2)}) async-start(), calls=%async_computation.3 | async-start | bytes 4055040 | tf_op jit(solution)/shard_map/all_gather | solution.py:246
  11.1 39.1 %collective-permute-start = (bf16[96,768]{1,0:T(8,128)(2,1)}, bf16[96,768]{1,0:T(8,128)(2,1)}, u32[]{:S(2)}, u32[]{:S(2)}) collective-permute-start(bf16[96,768]{1,0:T(8,128)(2,1)} %get-tuple-element.111), channel_id=1, source_target_pairs={{0,2},{1,3},{2,4},{3,5},{4,6},{5,7},{6,0},{7,1},{8,10},{9,11},{10,... | collective-permute-start | bytes 442376 | tf_op jit(solution)/shard_map/ppermute | solution.py:152
  14.1 36.1 %collective-permute-start.1 = (bf16[96,768]{1,0:T(8,128)(2,1)}, bf16[96,768]{1,0:T(8,128)(2,1)}, u32[]{:S(2)}, u32[]{:S(2)}) collective-permute-start(bf16[96,768]{1,0:T(8,128)(2,1)} %get-tuple-element.113), channel_id=1, source_target_pairs={{0,4},{1,5},{2,6},{3,7},{4,0},{5,1},{6,2},{7,3},{8,12},{9,13},{10,... | collective-permute-start | bytes 442376 | tf_op jit(solution)/shard_map/ppermute | solution.py:152
  16.7 33.5 %collective-permute-start.2 = (bf16[96,768]{1,0:T(8,128)(2,1)}, bf16[96,768]{1,0:T(8,128)(2,1)}, u32[]{:S(2)}, u32[]{:S(2)}) collective-permute-start(bf16[96,768]{1,0:T(8,128)(2,1)} %get-tuple-element.112), channel_id=1, source_target_pairs={{0,6},{1,7},{2,0},{3,1},{4,2},{5,3},{6,4},{7,5},{8,14},{9,15},{10,... | collective-permute-start | bytes 442376 | tf_op jit(solution)/shard_map/ppermute | solution.py:152
  45.8 7.6 %collective-permute-start.3 = (bf16[768,1152]{1,0:T(8,128)(2,1)}, bf16[768,1152]{1,0:T(8,128)(2,1)}, u32[]{:S(2)}, u32[]{:S(2)}) collective-permute-start(bf16[768,1152]{1,0:T(8,128)(2,1)} %all-gather.3.cloned.1.call-done), channel_id=1, source_target_pairs={{0,1},{1,0},{2,3},{3,2},{4,5},{5,4},{6,7},{7,6},{8,9},{9,8},{10,11... | collective-permute-start | bytes 5308424 | tf_op jit(solution)/shard_map/ppermute | solution.py:207
  46.7 153.8 %reduce-scatter.7.cloned.1.call-start = ((), (), s32[]{:S(2)}) async-start(), calls=%async_computation.7 | async-start | bytes 4055040
  50.2 10.1 %copy-start.2 = (f32[384,768]{1,0:T(8,128)}, f32[384,768]{1,0:T(8,128)S(1)}, u32[]{:S(2)}) copy-start(f32[384,768]{1,0:T(8,128)S(1)} %copy.25) | copy-start | bytes 3538948
  61.6 3.1 collective-permute-start.4
  93.0 15.8 %collective-permute-start.5 = (bf16[4,1056,384]{2,1,0:T(8,128)(2,1)}, bf16[4,1056,384]{2,1,0:T(8,128)(2,1)}, u32[]{:S(2)}, u32[]{:S(2)}) collective-permute-start(bf16[4,1056,384]{2,1,0:T(8,128)(2,1)} %all-gather.5.cloned.1.call-done), channel_id=1, source_target_pairs={{0,1},{1,0},{2,3},{3,2},{4,5},{5,4},{6,7},{7,6},{8,9},{9,8},{10,11... | collective-permute-start | bytes 9732104 | tf_op jit(solution)/shard_map/ppermute | solution.py:238
  94.2 10.8 %collective-permute-start.10 = (bf16[96,768]{1,0:T(8,128)(2,1)S(1)}, bf16[96,768]{1,0:T(8,128)(2,1)S(1)}, u32[]{:S(2)}, u32[]{:S(2)}) collective-permute-start(bf16[96,768]{1,0:T(8,128)(2,1)S(1)} %get-tuple-element.106), channel_id=1, source_target_pairs={{0,4},{1,5},{2,6},{3,7},{4,0},{5,1},{6,2},{7,3},{8,12},{9,13},{10,... | collective-permute-start | bytes 442376 | tf_op jit(solution)/shard_map/ppermute | solution.py:152
  96.6 8.3 %collective-permute-start.11 = (bf16[96,768]{1,0:T(8,128)(2,1)S(1)}, bf16[96,768]{1,0:T(8,128)(2,1)S(1)}, u32[]{:S(2)}, u32[]{:S(2)}) collective-permute-start(bf16[96,768]{1,0:T(8,128)(2,1)S(1)} %get-tuple-element.105), channel_id=1, source_target_pairs={{0,6},{1,7},{2,0},{3,1},{4,2},{5,3},{6,4},{7,5},{8,14},{9,15},{10,... | collective-permute-start | bytes 442376 | tf_op jit(solution)/shard_map/ppermute | solution.py:152
  98.1 10.7 %collective-permute-start.9 = (bf16[96,768]{1,0:T(8,128)(2,1)S(1)}, bf16[96,768]{1,0:T(8,128)(2,1)S(1)}, u32[]{:S(2)}, u32[]{:S(2)}) collective-permute-start(bf16[96,768]{1,0:T(8,128)(2,1)S(1)} %get-tuple-element.104), channel_id=1, source_target_pairs={{0,2},{1,3},{2,4},{3,5},{4,6},{5,7},{6,0},{7,1},{8,10},{9,11},{10,... | collective-permute-start | bytes 442376 | tf_op jit(solution)/shard_map/ppermute | solution.py:152
  105.0 13.0 %copy-start.28 = (bf16[96,768]{1,0:T(8,128)(2,1)}, bf16[96,768]{1,0:T(8,128)(2,1)S(1)}, u32[]{:S(2)}) copy-start(bf16[96,768]{1,0:T(8,128)(2,1)S(1)} %collective-permute-done.10) | copy-start | bytes 442372
  113.5 10.3 %copy-start.4 = (f32[384,768]{1,0:T(8,128)}, f32[384,768]{1,0:T(8,128)S(1)}, u32[]{:S(2)}) copy-start(f32[384,768]{1,0:T(8,128)S(1)} %get-tuple-element.117) | copy-start | bytes 3538948
  122.4 9.1 %collective-permute-start.14 = (bf16[768,1152]{1,0:T(8,128)(2,1)S(1)}, bf16[768,1152]{1,0:T(8,128)(2,1)S(1)}, u32[]{:S(2)}, u32[]{:S(2)}) collective-permute-start(bf16[768,1152]{1,0:T(8,128)(2,1)S(1)} %convolution_convert_fusion.1), channel_id=1, source_target_pairs={{0,1},{1,0},{2,3},{3,2},{4,5},{5,4},{6,7},{7,6},{8,9},{9,8},{10,11... | collective-permute-start | bytes 5308424 | tf_op jit(solution)/shard_map/ppermute | solution.py:211
  123.2 5.6 %collective-permute-start.12 = (bf16[1152,384]{1,0:T(8,128)(2,1)S(1)}, bf16[1152,384]{1,0:T(8,128)(2,1)S(1)}, u32[]{:S(2)}, u32[]{:S(2)}) collective-permute-start(bf16[1152,384]{1,0:T(8,128)(2,1)S(1)} %convolution_convert_fusion.2), channel_id=1, source_target_pairs={{0,1},{1,0},{2,3},{3,2},{4,5},{5,4},{6,7},{7,6},{8,9},{9,8},{10,11... | collective-permute-start | bytes 2654216 | tf_op jit(solution)/shard_map/ppermute | solution.py:211
  125.8 2.4 collective-permute-start.13
  135.4 81.6 %reduce-scatter.5.cloned.1.call-start = ((), (), s32[]{:S(2)}) async-start(), calls=%async_computation.4 | async-start | bytes 2211840 | tf_op jit(solution)/shard_map/reduce_scatter | solution.py:216
  152.9 2.9 collective-permute-start.15
  164.6 4.0 %collective-permute-start.19 = (bf16[768,1152]{1,0:T(8,128)(2,1)}, bf16[768,1152]{1,0:T(8,128)(2,1)}, u32[]{:S(2)}, u32[]{:S(2)}) collective-permute-start(bf16[768,1152]{1,0:T(8,128)(2,1)} %convolution_convert_fusion), channel_id=1, source_target_pairs={{0,1},{1,0},{2,3},{3,2},{4,5},{5,4},{6,7},{7,6},{8,9},{9,8},{10,11... | collective-permute-start | bytes 5308424 | tf_op jit(solution)/shard_map/ppermute | solution.py:211
  173.4 90.4 %all-reduce.4.cloned.1.call-start = ((), (), s32[]{:S(2)}) async-start(), calls=%async_computation.5 | async-start | bytes 1622016 | tf_op jit(solution)/shard_map/psum | solution.py:289
  173.5 6.6 %collective-permute-start.6 = (bf16[96,768]{1,0:T(8,128)(2,1)S(1)}, bf16[96,768]{1,0:T(8,128)(2,1)S(1)}, u32[]{:S(2)}, u32[]{:S(2)}) collective-permute-start(bf16[96,768]{1,0:T(8,128)(2,1)S(1)} %get-tuple-element.109), channel_id=1, source_target_pairs={{0,6},{1,7},{2,0},{3,1},{4,2},{5,3},{6,4},{7,5},{8,14},{9,15},{10,... | collective-permute-start | bytes 442376 | tf_op jit(solution)/shard_map/ppermute | solution.py:152
  175.6 15.6 %collective-permute-start.7 = (bf16[96,768]{1,0:T(8,128)(2,1)S(1)}, bf16[96,768]{1,0:T(8,128)(2,1)S(1)}, u32[]{:S(2)}, u32[]{:S(2)}) collective-permute-start(bf16[96,768]{1,0:T(8,128)(2,1)S(1)} %get-tuple-element.108), channel_id=1, source_target_pairs={{0,4},{1,5},{2,6},{3,7},{4,0},{5,1},{6,2},{7,3},{8,12},{9,13},{10,... | collective-permute-start | bytes 442376 | tf_op jit(solution)/shard_map/ppermute | solution.py:152
  177.7 13.6 %collective-permute-start.8 = (bf16[96,768]{1,0:T(8,128)(2,1)S(1)}, bf16[96,768]{1,0:T(8,128)(2,1)S(1)}, u32[]{:S(2)}, u32[]{:S(2)}) collective-permute-start(bf16[96,768]{1,0:T(8,128)(2,1)S(1)} %get-tuple-element.107), channel_id=1, source_target_pairs={{0,2},{1,3},{2,4},{3,5},{4,6},{5,7},{6,0},{7,1},{8,10},{9,11},{10,... | collective-permute-start | bytes 442376 | tf_op jit(solution)/shard_map/ppermute | solution.py:152
  198.2 6.8 %collective-permute-start.16 = (bf16[96,768]{1,0:T(8,128)(2,1)S(1)}, bf16[96,768]{1,0:T(8,128)(2,1)S(1)}, u32[]{:S(2)}, u32[]{:S(2)}) collective-permute-start(bf16[96,768]{1,0:T(8,128)(2,1)S(1)} %get-tuple-element.102), channel_id=1, source_target_pairs={{0,6},{1,7},{2,0},{3,1},{4,2},{5,3},{6,4},{7,5},{8,14},{9,15},{10,... | collective-permute-start | bytes 442376 | tf_op jit(solution)/shard_map/ppermute | solution.py:152
  198.2 13.7 %collective-permute-start.17 = (bf16[96,768]{1,0:T(8,128)(2,1)S(1)}, bf16[96,768]{1,0:T(8,128)(2,1)S(1)}, u32[]{:S(2)}, u32[]{:S(2)}) collective-permute-start(bf16[96,768]{1,0:T(8,128)(2,1)S(1)} %get-tuple-element.101), channel_id=1, source_target_pairs={{0,4},{1,5},{2,6},{3,7},{4,0},{5,1},{6,2},{7,3},{8,12},{9,13},{10,... | collective-permute-start | bytes 442376 | tf_op jit(solution)/shard_map/ppermute | solution.py:152
  198.5 13.5 %collective-permute-start.18 = (bf16[96,768]{1,0:T(8,128)(2,1)S(1)}, bf16[96,768]{1,0:T(8,128)(2,1)S(1)}, u32[]{:S(2)}, u32[]{:S(2)}) collective-permute-start(bf16[96,768]{1,0:T(8,128)(2,1)S(1)} %get-tuple-element.100), channel_id=1, source_target_pairs={{0,2},{1,3},{2,4},{3,5},{4,6},{5,7},{6,0},{7,1},{8,10},{9,11},{10,... | collective-permute-start | bytes 442376 | tf_op jit(solution)/shard_map/ppermute | solution.py:152
  200.5 102.0 %all-reduce.6.cloned.1.call-start = ((), (), s32[]{:S(2)}) async-start(), calls=%async_computation.6 | async-start | bytes 884736 | tf_op jit(solution)/shard_map/psum | solution.py:297
  263.8 38.8 %collective-permute-start.21 = (bf16[1,1056,384]{2,1,0:T(8,128)(2,1)}, bf16[1,1056,384]{2,1,0:T(8,128)(2,1)S(1)}, u32[]{:S(2)}, u32[]{:S(2)}) collective-permute-start(bf16[1,1056,384]{2,1,0:T(8,128)(2,1)} %all-reduce.4.cloned.1.call-done), channel_id=1, source_target_pairs={{0,1},{1,0},{2,3},{3,2},{4,5},{5,4},{6,7},{7,6},{8,9},{9,8},{10,11... | collective-permute-start | bytes 2433032 | tf_op jit(solution)/shard_map/ppermute | solution.py:238
  263.8 38.7 %copy-start.27 = (bf16[1,1056,384]{2,1,0:T(8,128)(2,1)S(1)}, bf16[1,1056,384]{2,1,0:T(8,128)(2,1)}, u32[]{:S(2)}) copy-start(bf16[1,1056,384]{2,1,0:T(8,128)(2,1)} %all-reduce.4.cloned.1.call-done) | copy-start | bytes 2433028
  302.6 2.0 collective-permute-start.20
  (41 other events, 106.6 us)
Sparse Core Ops, SparseCore 0:
  10.4 35.2 all-gather.2
  48.2 44.7 all-gather.4
  135.5 46.0 reduce-scatter.6
  184.5 32.4 reduce-scatter.4
  219.2 44.5 all-reduce.3
  266.0 36.5 all-reduce.5

commit v4 on v3

--- a/solution.py
+++ b/solution.py
@@ -286,16 +286,22 @@
     do = dot(dy, attn_all, NT).astype(bf16)
     part = pack(part_mlp, part_attn, part_in)
     do, part = lax.optimization_barrier((do, part))
-    part = lax.psum(scatter(part), "ctx", axis_index_groups=parity)
+    part = scatter(part)
     dq, dk, dv = attend_back(q, keys, values, do, lse)
     dk, dv = sum_keys(dk, dv)
     dqkv = jnp.concatenate(
         [unrotate(dq, cosines, sines), unrotate(dk, cosines, sines), dv], axis=-1
     ).astype(bf16)
     part_qkv = scatter(reduce_pair(h1, dqkv))
-    part_qkv, part = lax.optimization_barrier((part_qkv, part))
-    raw_qkv = both_halves(lax.psum(part_qkv, "ctx", axis_index_groups=parity)).astype(f32)
-    grad_mlp, grad_attn, raw_in = [t.astype(f32) for t in join_packed(part)]
+    blocks = [part_qkv[None, :, i : i + narrow] for i in range(0, part_qkv.shape[1], narrow)]
+    part = lax.psum(jnp.concatenate([part] + blocks, axis=1), "ctx", axis_index_groups=parity)
+    other = lax.ppermute(part, "ctx", swap)
+    (mlp_own, attn_own, wide_own), (mlp_got, attn_got, wide_got) = unpack(part), unpack(other)
+    grad_mlp = join(mlp_own, mlp_got).astype(f32)
+    grad_attn = join(attn_own, attn_got).astype(f32)
+    middle = w_in.shape[1] // 2
+    raw_in = join(wide_own[:, :middle], wide_got[:, :middle]).astype(f32)
+    raw_qkv = join(wide_own[:, middle:], wide_got[:, middle:]).astype(f32)
     dx = dx2 + norm_back(dot(dqkv, qkv_all, NT), xhat, scale_one)
     grad_tokens = from_sequence(dx.astype(bf16)).astype(f32)
     return (

time: 318 us -> 342 us (1.075)
  waiting for transfers between devices: 172 us -> 192 us
  matrix products: 30.3 us -> 26.4 us
    unnamed x7 -> x6, waiting for transfers between devices: 0.12 us -> 47.1 us
    psum x2 -> x1, waiting for transfers between devices: 84.4 us -> 41.2 us  [body(): lax.psum(jnp.concatenate([part] + blocks, axis=1), 'ctx', axis_index_grou...]
    ppermute x12, waiting for transfers between devices: 33.1 us -> 43.3 us  [hop(): return lax.ppermute(block, 'ctx', route)]
    dot_general x16, matrix products: 30.3 us -> 26.4 us  [dot(): return lax.dot_general(a, b, (dims, ((), ())), preferred_element_type=f32)]
    unnamed x112 -> x98, local copies, waits for them, and re-layouts: 11.7 us -> 13.9 us
  transfers between devices with their start and end apart: 28 -> 26, of which waited for: 15 -> 16; matrix products, arithmetic and copies ran while one was open for 16% -> 10% of each run, Pallas kernels for 8% -> 3%
where the time goes in v4:
time: 342 us; the launch traced here: 341 us
  waiting for transfers between devices  192 us (56%)
  other arithmetic  33.2 us (10%)
  matrix products  26.4 us (8%)
  Pallas kernels  25.8 us (8%)
  starting transfers between devices  24.6 us (7%)
  local copies, waits for them, and re-layouts  23.9 us (7%)
  between operations  14.9 us (4%)
    unnamed x6, waiting for transfers between devices  47.1 us
    ppermute x12, waiting for transfers between devices, hop(): return lax.ppermute(block, 'ctx', route)  43.3 us
    psum x1, waiting for transfers between devices, body(): lax.psum(jnp.concatenate([part] + blocks, axis=1), 'ctx', axis_index_grou...  41.2 us
    dot_general x16, matrix products, dot(): return lax.dot_general(a, b, (dims, ((), ())), preferred_element_type=f32)  26.4 us
    all_gather x1, waiting for transfers between devices, gather(): return lax.all_gather(half_of(shard, core), 'seq', axis=0, tiled=True)  25.5 us
    ppermute x12, starting transfers between devices, hop(): return lax.ppermute(block, 'ctx', route)  22.6 us
    pallas_call x1, Pallas kernels, attend_back(): pl.pallas_call(attend_back_kernel, grid=(width // PAIR,), in_specs=[colum...  15.9 us
    all_gather x1, waiting for transfers between devices, body(): packed = lax.all_gather(packed, 'seq', axis=0, tiled=True)  15.8 us
  transfers between devices with their start and end apart: 26, of which 16 were waited for; matrix products, arithmetic and copies ran while one was open for 10% of the time, Pallas kernels for 3%

profile of v4, /device:TPU:0, one launch (start us, length us, event | category | flops | bytes accessed | tf_op | source)
XLA Modules:
  0.0 341.1 jit_solution(11271773642222307058)
XLA Ops:
  11.1 3.0 collective-permute-start
  14.1 2.6 collective-permute-start.1
  20.3 25.5 %all-gather.3.cloned.1.call-done = bf16[768,1152]{1,0:T(8,128)(2,1)} async-done(((bf16[192,1152]{1,0:T(8,128)(2,1)}), bf16[768,1152]{1,0:T(8,128)(2,1)}) %all-gather.3.cloned.1.call-update) | async-done | bytes 1769488 | tf_op jit(solution)/shard_map/all_gather | solution.py:204
  53.4 2.6 broadcast_select_fusion.3
  56.0 3.2 fusion.4
  62.3 2.4 collective-permute-done.4
  66.3 9.9 %shard_map.143 = (bf16[384,768]{1,0:T(8,128)(2,1)S(1)}, f32[384,768]{1,0:T(8,128)S(1)}) custom-call(bf16[384,768]{1,0:T(8,128)(2,1)S(1)} %get-tuple-element.37.q_ref, bf16[768,768]{1,0:T(8,128)(2,1)S(1)} %pad_maximum_fusion.14.k_ref, bf16[768,768]{1,0:T(8,128)(2,1)} %pad_maximum_fusion.15.v_ref), custom_call_target="tpu_custom_call" | custom-call | flops 905969664 | bytes 7077888 | tf_op jit(solution)/shard_map/pallas_call | solution.py:69
  77.2 15.8 %all-gather.5.cloned.1.call-done = bf16[4,1056,384]{2,1,0:T(8,128)(2,1)} async-done(((bf16[1,1056,384]{2,1,0:T(8,128)(2,1)}), bf16[4,1056,384]{2,1,0:T(8,128)(2,1)}) %all-gather.5.cloned.1.call-update) | async-done | bytes 3244048 | tf_op jit(solution)/shard_map/all_gather | solution.py:246
  94.2 2.5 collective-permute-start.10
  98.7 6.3 %collective-permute-done.10 = bf16[96,768]{1,0:T(8,128)(2,1)S(1)} collective-permute-done((bf16[96,768]{1,0:T(8,128)(2,1)S(1)}, bf16[96,768]{1,0:T(8,128)(2,1)S(1)}, u32[]{:S(2)}, u32[]{:S(2)}) %collective-permute-start.10) | collective-permute-done | bytes 147488 | tf_op jit(solution)/shard_map/ppermute | solution.py:152
  105.0 3.8 %collective-permute-done.9 = bf16[96,768]{1,0:T(8,128)(2,1)S(1)} collective-permute-done((bf16[96,768]{1,0:T(8,128)(2,1)S(1)}, bf16[96,768]{1,0:T(8,128)(2,1)S(1)}, u32[]{:S(2)}, u32[]{:S(2)}) %collective-permute-start.9) | collective-permute-done | bytes 147488 | tf_op jit(solution)/shard_map/ppermute | solution.py:152
  108.8 2.8 fusion.103
  135.2 15.9 %shard_map.144 = (f32[384,768]{1,0:T(8,128)S(1)}, bf16[768,768]{1,0:T(8,128)(2,1)S(1)}, bf16[768,768]{1,0:T(8,128)(2,1)}) custom-call(bf16[384,768]{1,0:T(8,128)(2,1)S(1)} %get-tuple-element.37.q_ref, bf16[768,768]{1,0:T(8,128)(2,1)} %copy-done, bf16[768,768]{1,0:T(8,128)(2,1)} %pad_maximum_fusion.15.v_ref, ...), custom_call_target="tpu_custom_call" | custom-call | flops 2264924160 | bytes 10616832 | tf_op jit(solution)/shard_map/pallas_call | solution.py:90
  152.7 2.7 collective-permute-done.15
  159.5 2.4 convolution_convert_fusion
  162.1 3.5 %collective-permute-done.19 = bf16[768,1152]{1,0:T(8,128)(2,1)S(1)} collective-permute-done((bf16[768,1152]{1,0:T(8,128)(2,1)S(1)}, bf16[768,1152]{1,0:T(8,128)(2,1)S(1)}, u32[]{:S(2)}, u32[]{:S(2)}) %collective-permute-start.19) | collective-permute-done | bytes 1769504 | tf_op jit(solution)/shard_map/ppermute | solution.py:211
  165.7 3.6 %add_convert_fusion = bf16[768,1152]{1,0:T(8,128)(2,1)} fusion(bf16[768,1152]{1,0:T(8,128)(2,1)S(1)} %collective-permute-done.19, bf16[384,2304]{1,0:T(8,128)(2,1)S(1)} %pad_maximum_fusion.11, s32[]{:T(128)S(6)} %select_n.241, f32[384]{0:T(512)S(1)} %add_rsqrt_fusion.1, f32[384]{0:T(512)S(1)} %broadcast_multiply_fusion.5, ...), kind=kOutput, calls=%fused_computation.2 | convolution fusion | flops 685375488 | bytes 5017604 | tf_op jit(solution)/shard_map/dot_general | solution.py:22
  171.1 2.2 fusion.18
  173.4 2.6 collective-permute-start.6
  176.0 2.1 collective-permute-start.7
  178.1 1.9 collective-permute-start.8
  180.3 11.3 %collective-permute-done.7 = bf16[96,768]{1,0:T(8,128)(2,1)S(1)} collective-permute-done((bf16[96,768]{1,0:T(8,128)(2,1)S(1)}, bf16[96,768]{1,0:T(8,128)(2,1)S(1)}, u32[]{:S(2)}, u32[]{:S(2)}) %collective-permute-start.7) | collective-permute-done | bytes 147488 | tf_op jit(solution)/shard_map/ppermute | solution.py:152
  193.2 2.8 fusion.98
  196.0 7.1 %reduce-scatter.5.cloned.1.call-done = bf16[192,1152]{1,0:T(8,128)(2,1)} async-done(((bf16[768,1152]{1,0:T(8,128)(2,1)}), bf16[192,1152]{1,0:T(8,128)(2,1)}) %reduce-scatter.5.cloned.1.call-update) | async-done | bytes 442384 | tf_op jit(solution)/shard_map/reduce_scatter | solution.py:216
  204.3 46.5 %reduce-scatter.7.cloned.1.call-done = bf16[1,1056,384]{2,1,0:T(8,128)(2,1)} async-done(((bf16[4,1056,384]{2,1,0:T(8,128)(2,1)}), bf16[1,1056,384]{2,1,0:T(8,128)(2,1)}) %reduce-scatter.7.cloned.1.call-update) | async-done | bytes 811024
  250.8 2.3 pad_maximum_fusion.12
  255.9 3.4 collective-permute-start.16
  260.4 6.1 %collective-permute-done.16 = bf16[96,768]{1,0:T(8,128)(2,1)S(1)} collective-permute-done((bf16[96,768]{1,0:T(8,128)(2,1)S(1)}, bf16[96,768]{1,0:T(8,128)(2,1)S(1)}, u32[]{:S(2)}, u32[]{:S(2)}) %collective-permute-start.16) | collective-permute-done | bytes 147488 | tf_op jit(solution)/shard_map/ppermute | solution.py:152
  266.5 15.5 %collective-permute-done.17 = bf16[96,768]{1,0:T(8,128)(2,1)S(1)} collective-permute-done((bf16[96,768]{1,0:T(8,128)(2,1)S(1)}, bf16[96,768]{1,0:T(8,128)(2,1)S(1)}, u32[]{:S(2)}, u32[]{:S(2)}) %collective-permute-start.17) | collective-permute-done | bytes 147488 | tf_op jit(solution)/shard_map/ppermute | solution.py:152
  282.0 41.2 %all-reduce.3.cloned.1.call-done = bf16[1,1632,384]{2,1,0:T(8,128)(2,1)} async-done(((bf16[1,1632,384]{2,1,0:T(8,128)(2,1)}), bf16[1,1632,384]{2,1,0:T(8,128)(2,1)}) %all-reduce.3.cloned.1.call-update) | async-done | bytes 1253392 | tf_op jit(solution)/shard_map/psum | solution.py:297
  328.8 2.2 fusion.6
  332.4 2.2 fusion.5
  (216 shorter events, 68.1 us)
Async XLA Ops:
  7.2 38.6 %all-gather.3.cloned.1.call-start = ((), (), s32[]{:S(2)}) async-start(), calls=%async_computation.2 | async-start | bytes 2211840 | tf_op jit(solution)/shard_map/all_gather | solution.py:204
  10.1 8.0 %copy-start.7 = (bf16[192,2304]{1,0:T(8,128)(2,1)S(1)}, bf16[192,2304]{1,0:T(8,128)(2,1)}, u32[]{:S(2)}) copy-start(bf16[192,2304]{1,0:T(8,128)(2,1)} %param.11) | copy-start | bytes 2654212
  10.1 82.9 %all-gather.5.cloned.1.call-start = ((), (), s32[]{:S(2)}) async-start(), calls=%async_computation.3 | async-start | bytes 4055040 | tf_op jit(solution)/shard_map/all_gather | solution.py:246
  11.1 39.1 %collective-permute-start = (bf16[96,768]{1,0:T(8,128)(2,1)}, bf16[96,768]{1,0:T(8,128)(2,1)}, u32[]{:S(2)}, u32[]{:S(2)}) collective-permute-start(bf16[96,768]{1,0:T(8,128)(2,1)} %get-tuple-element.113), channel_id=1, source_target_pairs={{0,2},{1,3},{2,4},{3,5},{4,6},{5,7},{6,0},{7,1},{8,10},{9,11},{10,... | collective-permute-start | bytes 442376 | tf_op jit(solution)/shard_map/ppermute | solution.py:152
  14.1 36.1 %collective-permute-start.1 = (bf16[96,768]{1,0:T(8,128)(2,1)}, bf16[96,768]{1,0:T(8,128)(2,1)}, u32[]{:S(2)}, u32[]{:S(2)}) collective-permute-start(bf16[96,768]{1,0:T(8,128)(2,1)} %get-tuple-element.115), channel_id=1, source_target_pairs={{0,4},{1,5},{2,6},{3,7},{4,0},{5,1},{6,2},{7,3},{8,12},{9,13},{10,... | collective-permute-start | bytes 442376 | tf_op jit(solution)/shard_map/ppermute | solution.py:152
  16.7 33.5 %collective-permute-start.2 = (bf16[96,768]{1,0:T(8,128)(2,1)}, bf16[96,768]{1,0:T(8,128)(2,1)}, u32[]{:S(2)}, u32[]{:S(2)}) collective-permute-start(bf16[96,768]{1,0:T(8,128)(2,1)} %get-tuple-element.114), channel_id=1, source_target_pairs={{0,6},{1,7},{2,0},{3,1},{4,2},{5,3},{6,4},{7,5},{8,14},{9,15},{10,... | collective-permute-start | bytes 442376 | tf_op jit(solution)/shard_map/ppermute | solution.py:152
  45.8 7.6 %collective-permute-start.3 = (bf16[768,1152]{1,0:T(8,128)(2,1)}, bf16[768,1152]{1,0:T(8,128)(2,1)}, u32[]{:S(2)}, u32[]{:S(2)}) collective-permute-start(bf16[768,1152]{1,0:T(8,128)(2,1)} %all-gather.3.cloned.1.call-done), channel_id=1, source_target_pairs={{0,1},{1,0},{2,3},{3,2},{4,5},{5,4},{6,7},{7,6},{8,9},{9,8},{10,11... | collective-permute-start | bytes 5308424 | tf_op jit(solution)/shard_map/ppermute | solution.py:207
  46.7 156.5 %reduce-scatter.5.cloned.1.call-start = ((), (), s32[]{:S(2)}) async-start(), calls=%async_computation.4 | async-start | bytes 2211840 | tf_op jit(solution)/shard_map/reduce_scatter | solution.py:216
  50.2 10.1 %copy-start.2 = (f32[384,768]{1,0:T(8,128)}, f32[384,768]{1,0:T(8,128)S(1)}, u32[]{:S(2)}) copy-start(f32[384,768]{1,0:T(8,128)S(1)} %copy.25) | copy-start | bytes 3538948
  61.6 3.1 collective-permute-start.4
  93.0 15.8 %collective-permute-start.5 = (bf16[4,1056,384]{2,1,0:T(8,128)(2,1)}, bf16[4,1056,384]{2,1,0:T(8,128)(2,1)}, u32[]{:S(2)}, u32[]{:S(2)}) collective-permute-start(bf16[4,1056,384]{2,1,0:T(8,128)(2,1)} %all-gather.5.cloned.1.call-done), channel_id=1, source_target_pairs={{0,1},{1,0},{2,3},{3,2},{4,5},{5,4},{6,7},{7,6},{8,9},{9,8},{10,11... | collective-permute-start | bytes 9732104 | tf_op jit(solution)/shard_map/ppermute | solution.py:238
  94.2 10.8 %collective-permute-start.10 = (bf16[96,768]{1,0:T(8,128)(2,1)S(1)}, bf16[96,768]{1,0:T(8,128)(2,1)S(1)}, u32[]{:S(2)}, u32[]{:S(2)}) collective-permute-start(bf16[96,768]{1,0:T(8,128)(2,1)S(1)} %get-tuple-element.108), channel_id=1, source_target_pairs={{0,4},{1,5},{2,6},{3,7},{4,0},{5,1},{6,2},{7,3},{8,12},{9,13},{10,... | collective-permute-start | bytes 442376 | tf_op jit(solution)/shard_map/ppermute | solution.py:152
  96.6 8.3 %collective-permute-start.11 = (bf16[96,768]{1,0:T(8,128)(2,1)S(1)}, bf16[96,768]{1,0:T(8,128)(2,1)S(1)}, u32[]{:S(2)}, u32[]{:S(2)}) collective-permute-start(bf16[96,768]{1,0:T(8,128)(2,1)S(1)} %get-tuple-element.107), channel_id=1, source_target_pairs={{0,6},{1,7},{2,0},{3,1},{4,2},{5,3},{6,4},{7,5},{8,14},{9,15},{10,... | collective-permute-start | bytes 442376 | tf_op jit(solution)/shard_map/ppermute | solution.py:152
  98.1 10.7 %collective-permute-start.9 = (bf16[96,768]{1,0:T(8,128)(2,1)S(1)}, bf16[96,768]{1,0:T(8,128)(2,1)S(1)}, u32[]{:S(2)}, u32[]{:S(2)}) collective-permute-start(bf16[96,768]{1,0:T(8,128)(2,1)S(1)} %get-tuple-element.106), channel_id=1, source_target_pairs={{0,2},{1,3},{2,4},{3,5},{4,6},{5,7},{6,0},{7,1},{8,10},{9,11},{10,... | collective-permute-start | bytes 442376 | tf_op jit(solution)/shard_map/ppermute | solution.py:152
  113.5 10.2 %copy-start.4 = (f32[384,768]{1,0:T(8,128)}, f32[384,768]{1,0:T(8,128)S(1)}, u32[]{:S(2)}) copy-start(f32[384,768]{1,0:T(8,128)S(1)} %get-tuple-element.122) | copy-start | bytes 3538948
  119.2 9.4 %copy-start.37 = (bf16[384,1152]{1,0:T(8,128)(2,1)}, bf16[384,1152]{1,0:T(8,128)(2,1)S(1)}, u32[]{:S(2)}) copy-start(bf16[384,1152]{1,0:T(8,128)(2,1)S(1)} %get-tuple-element.40) | copy-start | bytes 2654212
  122.2 9.1 %collective-permute-start.14 = (bf16[768,1152]{1,0:T(8,128)(2,1)S(1)}, bf16[768,1152]{1,0:T(8,128)(2,1)S(1)}, u32[]{:S(2)}, u32[]{:S(2)}) collective-permute-start(bf16[768,1152]{1,0:T(8,128)(2,1)S(1)} %convolution_convert_fusion.1), channel_id=1, source_target_pairs={{0,1},{1,0},{2,3},{3,2},{4,5},{5,4},{6,7},{7,6},{8,9},{9,8},{10,11... | collective-permute-start | bytes 5308424 | tf_op jit(solution)/shard_map/ppermute | solution.py:211
  123.1 5.6 %collective-permute-start.12 = (bf16[1152,384]{1,0:T(8,128)(2,1)S(1)}, bf16[1152,384]{1,0:T(8,128)(2,1)S(1)}, u32[]{:S(2)}, u32[]{:S(2)}) collective-permute-start(bf16[1152,384]{1,0:T(8,128)(2,1)S(1)} %convolution_convert_fusion.2), channel_id=1, source_target_pairs={{0,1},{1,0},{2,3},{3,2},{4,5},{5,4},{6,7},{7,6},{8,9},{9,8},{10,11... | collective-permute-start | bytes 2654216 | tf_op jit(solution)/shard_map/ppermute | solution.py:211
  125.7 2.4 collective-permute-start.13
  152.4 2.9 collective-permute-start.15
  161.9 3.8 %collective-permute-start.19 = (bf16[768,1152]{1,0:T(8,128)(2,1)S(1)}, bf16[768,1152]{1,0:T(8,128)(2,1)S(1)}, u32[]{:S(2)}, u32[]{:S(2)}) collective-permute-start(bf16[768,1152]{1,0:T(8,128)(2,1)S(1)} %convolution_convert_fusion), channel_id=1, source_target_pairs={{0,1},{1,0},{2,3},{3,2},{4,5},{5,4},{6,7},{7,6},{8,9},{9,8},{10,11... | collective-permute-start | bytes 5308424 | tf_op jit(solution)/shard_map/ppermute | solution.py:211
  169.3 81.5 %reduce-scatter.7.cloned.1.call-start = ((), (), s32[]{:S(2)}) async-start(), calls=%async_computation.6 | async-start | bytes 4055040
  169.9 153.3 %all-reduce.3.cloned.1.call-start = ((), (), s32[]{:S(2)}) async-start(), calls=%async_computation.5 | async-start | bytes 2506752 | tf_op jit(solution)/shard_map/psum | solution.py:297
  171.1 21.6 %copy-start.20 = (bf16[768,1152]{1,0:T(8,128)(2,1)S(1)}, bf16[768,1152]{1,0:T(8,128)(2,1)}, u32[]{:S(2)}) copy-start(bf16[768,1152]{1,0:T(8,128)(2,1)} %copy-done.19) | copy-start | bytes 5308420
  173.3 19.3 %copy-start.18 = (bf16[768,1152]{1,0:T(8,128)(2,1)S(1)}, bf16[768,1152]{1,0:T(8,128)(2,1)}, u32[]{:S(2)}) copy-start(bf16[768,1152]{1,0:T(8,128)(2,1)} %copy-done.17) | copy-start | bytes 5308420
  173.4 6.9 %collective-permute-start.6 = (bf16[96,768]{1,0:T(8,128)(2,1)S(1)}, bf16[96,768]{1,0:T(8,128)(2,1)S(1)}, u32[]{:S(2)}, u32[]{:S(2)}) collective-permute-start(bf16[96,768]{1,0:T(8,128)(2,1)S(1)} %get-tuple-element.111), channel_id=1, source_target_pairs={{0,6},{1,7},{2,0},{3,1},{4,2},{5,3},{6,4},{7,5},{8,14},{9,15},{10,... | collective-permute-start | bytes 442376 | tf_op jit(solution)/shard_map/ppermute | solution.py:152
  176.0 15.7 %collective-permute-start.7 = (bf16[96,768]{1,0:T(8,128)(2,1)S(1)}, bf16[96,768]{1,0:T(8,128)(2,1)S(1)}, u32[]{:S(2)}, u32[]{:S(2)}) collective-permute-start(bf16[96,768]{1,0:T(8,128)(2,1)S(1)} %get-tuple-element.110), channel_id=1, source_target_pairs={{0,4},{1,5},{2,6},{3,7},{4,0},{5,1},{6,2},{7,3},{8,12},{9,13},{10,... | collective-permute-start | bytes 442376 | tf_op jit(solution)/shard_map/ppermute | solution.py:152
  178.1 13.6 %collective-permute-start.8 = (bf16[96,768]{1,0:T(8,128)(2,1)S(1)}, bf16[96,768]{1,0:T(8,128)(2,1)S(1)}, u32[]{:S(2)}, u32[]{:S(2)}) collective-permute-start(bf16[96,768]{1,0:T(8,128)(2,1)S(1)} %get-tuple-element.109), channel_id=1, source_target_pairs={{0,2},{1,3},{2,4},{3,5},{4,6},{5,7},{6,0},{7,1},{8,10},{9,11},{10,... | collective-permute-start | bytes 442376 | tf_op jit(solution)/shard_map/ppermute | solution.py:152
  255.9 10.6 %collective-permute-start.16 = (bf16[96,768]{1,0:T(8,128)(2,1)S(1)}, bf16[96,768]{1,0:T(8,128)(2,1)S(1)}, u32[]{:S(2)}, u32[]{:S(2)}) collective-permute-start(bf16[96,768]{1,0:T(8,128)(2,1)S(1)} %get-tuple-element.104), channel_id=1, source_target_pairs={{0,6},{1,7},{2,0},{3,1},{4,2},{5,3},{6,4},{7,5},{8,14},{9,15},{10,... | collective-permute-start | bytes 442376 | tf_op jit(solution)/shard_map/ppermute | solution.py:152
  259.3 22.7 %collective-permute-start.17 = (bf16[96,768]{1,0:T(8,128)(2,1)S(1)}, bf16[96,768]{1,0:T(8,128)(2,1)S(1)}, u32[]{:S(2)}, u32[]{:S(2)}) collective-permute-start(bf16[96,768]{1,0:T(8,128)(2,1)S(1)} %get-tuple-element.103), channel_id=1, source_target_pairs={{0,4},{1,5},{2,6},{3,7},{4,0},{5,1},{6,2},{7,3},{8,12},{9,13},{10,... | collective-permute-start | bytes 442376 | tf_op jit(solution)/shard_map/ppermute | solution.py:152
  259.3 64.0 %collective-permute-start.18 = (bf16[96,768]{1,0:T(8,128)(2,1)S(1)}, bf16[96,768]{1,0:T(8,128)(2,1)S(1)}, u32[]{:S(2)}, u32[]{:S(2)}) collective-permute-start(bf16[96,768]{1,0:T(8,128)(2,1)S(1)} %get-tuple-element.102), channel_id=1, source_target_pairs={{0,2},{1,3},{2,4},{3,5},{4,6},{5,7},{6,0},{7,1},{8,10},{9,11},{10,... | collective-permute-start | bytes 442376 | tf_op jit(solution)/shard_map/ppermute | solution.py:152
  323.2 3.2 collective-permute-start.20
  (32 other events, 57.6 us)
Sparse Core Ops, SparseCore 0:
  10.4 35.2 all-gather.2
  48.2 44.7 all-gather.4
  169.4 33.6 reduce-scatter.4
  206.0 44.7 reduce-scatter.6
  253.6 69.4 all-reduce.2
